TPU v7x, 32 devices: a whole 2x2x4 slice. The times are simulated.
32 devices in a mesh: expert: 8 (over z, y), shard: 4 (over x, core).
Axes of the slice: x: 2, y: 2, z: 4, core: 2. Of those that a mesh axis runs over, the one named last changes fastest.
Arguments:
- tokens: bfloat16 [20480, 768], P(('expert', 'shard')), may hold values from -6 to 6
- gain_attn: bfloat16 [768], P('shard'), may hold values from 0.5 to 1.5
- w_query: bfloat16 [768, 768], P('shard'), may hold values from -0.21875 to 0.21875
- w_key: bfloat16 [768, 768], P('shard'), may hold values from -0.21875 to 0.21875
- w_value: bfloat16 [768, 768], P('shard'), may hold values from -0.21875 to 0.21875
- w_output: bfloat16 [768, 768], P('shard'), may hold values from -1.75 to 1.75
- rel_table: bfloat16 [12, 16], P('shard'), may hold values from -4 to 4
- gain_moe: bfloat16 [768], P('shard'), may hold values from 0.5 to 1.5
- router: bfloat16 [768, 8], P('shard'), may hold values from -0.15625 to 0.15625
- w_in: bfloat16 [8, 768, 3072], P('expert', 'shard'), may hold values from -0.21875 to 0.21875
- w_out: bfloat16 [8, 3072, 768], P('expert', 'shard'), may hold values from -0.15625 to 0.15625
- routes: int32 [20480, 2], P(('expert', 'shard')), may hold values from 0 to 7, all different within a row; in each aligned block of 640 rows (0 to 639, 640 to 1279, ...) at most 228 rows name the same one
- parents: int32 [8, 20], P('expert'), may hold values from -1 to 19, as said below
- cotangent: bfloat16 [20480, 768], P(('expert', 'shard')), may hold values from -6 to 6
Outputs:
- output: bfloat16 [20480, 768], P(('expert', 'shard'))
- grad_tokens: bfloat16 [20480, 768], P(('expert', 'shard'))
- grad_gain_attn: float32 [768], P('shard')
- grad_w_query: float32 [768, 768], P('shard')
- grad_w_key: float32 [768, 768], P('shard')
- grad_w_value: float32 [768, 768], P('shard')
- grad_w_output: float32 [768, 768], P('shard')
- grad_table: float32 [12, 16], P('shard')
- grad_gain_moe: float32 [768], P('shard')
- grad_router: float32 [768, 8], P('shard')
- grad_w_in: float32 [8, 768, 3072], P('expert', 'shard')
- grad_w_out: float32 [8, 3072, 768], P('expert', 'shard')
Inputs may be any that keep to these rules, and one draw needn't show every extreme that they name: `routes`: in each aligned block of 640 rows (the tokens of one device) no expert is named by more than 228 rows; the two ids of a row differ. `parents`: segments 0 to 7 form the trunk: segment 0 is the root (parent -1) and each trunk segment is the parent of the next. 4 other segments, the last segment always among them, have segment 8 - 1 as parent; each of them is the parent of 2 of the remaining segments.
All inputs are finite; a program needn't handle non-finite values.
Results may differ from a plain program's by a relative error of at most 0.018.
Values may be sent and summed in bfloat16 or wider, within the bound.
No kernel may reach another device: no remote copies, remote signals or barrier semaphores. Data moves between devices by JAX's collectives and lax.ppermute only.
A program may use at most 192 MiB of HBM per device.

v0:
```python
import functools
import math

import jax
import jax.numpy as jnp
from jax import lax
from jax.experimental import pallas as pl
from jax.experimental.pallas import tpu as pltpu
from jax.sharding import PartitionSpec as P

DH = 64
NB = 16
SEG = 128
SEGS = 20
TRUNK = 8
SPARE = 3

THRESHOLDS = (1, 2, 3, 4, 5, 6, 7, 8, 12, 16, 24, 32, 48, 64, 96)
EPS = 1e-06
MASKED = -1e30
HW = 256

F32 = jnp.float32
BF16 = jnp.bfloat16
VMEM = pl.BlockSpec(memory_space=pltpu.VMEM)
SMEM = pl.BlockSpec(memory_space=pltpu.SMEM)
ANY = pl.BlockSpec(memory_space=pl.ANY)

NN = ((1,), (0,))
NT = ((1,), (1,))
TN = ((0,), (0,))


def params(mib=60, **more):
    return pltpu.CompilerParams(vmem_limit_bytes=mib << 20, **more)


SHORT = pl.CostEstimate(flops=0, bytes_accessed=1024, transcendentals=0)
LONG = pl.CostEstimate(flops=1 << 40, bytes_accessed=1 << 32, transcendentals=0)


FORWARD = pl.CostEstimate(flops=30_400_000_000, bytes_accessed=1024, transcendentals=0)
BACKWARD = pl.CostEstimate(flops=22_000_000_000, bytes_accessed=1024, transcendentals=0)


def dot(left, right, contract):
    return lax.dot_general(left, right, (contract, ((), ())), preferred_element_type=F32)


def arrays(*shapes):
    return [jax.ShapeDtypeStruct(shape, dtype) for shape, dtype in shapes]


def rms_parts(values):
    factor = lax.rsqrt(jnp.mean(values * values, axis=-1, keepdims=True) + EPS)
    return values * factor, factor


def rms_grad(grad_out, gain_row, unit_rows, factor):
    scaled = grad_out * gain_row
    return factor * (scaled - unit_rows * jnp.mean(scaled * unit_rows, axis=-1, keepdims=True))


def columns_kernel(me_ref, q_ref, k_ref, v_ref, more_ref, *out_refs):
    groups = len(out_refs)
    depth, width = out_refs[0].shape
    hw = q_ref.shape[1] // groups
    blocks = [
        jnp.concatenate([ref[:, s * hw:(s + 1) * hw] for ref in (q_ref, k_ref, v_ref)], axis=1) for s in range(groups)
    ]
    more = jnp.concatenate(
        [more_ref[...], jnp.zeros((depth, width - 3 * hw - more_ref.shape[1]), BF16)], axis=1
    )
    for bit in (1, 2):
        swapped = (me_ref[0] & bit) != 0
        blocks = [jnp.where(swapped, blocks[i ^ bit], blocks[i]) for i in range(groups)]
    for block, out_ref in zip(blocks, out_refs):
        out_ref[...] = jnp.concatenate([block, more], axis=1)


def project_kernel(
    heads, me_ref, table_ref, w0, w1, w2, w3, t0, t1, t2, t3, before_ref,
    n_ref, q_ref, k_ref, v_ref, kt_ref, vt_ref, w_ref, bias_ref, gain_ref, gain_two_ref, router_ref, w_pad,
):
    step = pl.program_id(0)

    @pl.when(step == 0)
    def _():
        hw = heads * DH
        blank = jnp.zeros((w0.shape[0], HW - hw), BF16)
        for rel, piece_ref in enumerate((w0, w1, w2, w3)):
            depth = piece_ref.shape[0]
            at = pl.ds(pl.multiple_of(jnp.bitwise_xor(me_ref[0], rel) * depth, 16), depth)
            piece = piece_ref[...]
            blank_end = jnp.zeros((depth, w_ref.shape[1] - 3 * hw), BF16)
            w_ref[at, :] = jnp.concatenate([piece[:, :3 * hw], blank_end], axis=1)
            router_ref[at, :] = piece[:, 3 * hw + 2:3 * hw + 2 + router_ref.shape[1]]
            padded = [part for c in range(3) for part in (piece[:, c * hw:(c + 1) * hw], blank)]
            padded.append(piece[:, 3 * hw:3 * hw + 2])
            padded.append(jnp.zeros((depth, w_pad.shape[1] - 3 * HW - 2), BF16))
            w_pad[at, :] = jnp.concatenate(padded, axis=1)
        gains = jnp.transpose(w_pad[:, 3 * HW:].astype(F32))
        gain_ref[...] = gains[0:1]
        gain_two_ref[...] = gains[1:2]
        key = lax.broadcasted_iota(jnp.int32, (SEG, SEG), 0)
        query = lax.broadcasted_iota(jnp.int32, (SEG, SEG), 1)
        bias_ref[0] = jnp.zeros((SEG, heads * SEG), F32)
        bias_ref[3] = jnp.full((SEG, heads * SEG), MASKED, F32)
        for h in range(heads):
            last = table_ref[h, NB - 1]
            at = slice(h * SEG, (h + 1) * SEG)
            for kind, gap in ((1, query - key + SEG), (2, query - key)):
                tile = jnp.zeros((SEG, SEG), F32) + (table_ref[h, 0] - last)
                for i, threshold in enumerate(THRESHOLDS):
                    tile = jnp.where(gap >= threshold, table_ref[h, i + 1] - last, tile)
                bias_ref[kind, :, at] = jnp.where(gap >= 0, tile, MASKED)

    for rel, t_ref in enumerate((t0, t1, t2, t3)):
        @pl.when(step == rel)
        def _(t_ref=t_ref):
            unit, _ = rms_parts(t_ref[...].astype(F32))
            normed = (unit * gain_ref[...]).astype(BF16)
            n_ref[0] = normed
            qkv = dot(normed, w_pad[:, :3 * HW], NN)
            q_ref[...] = qkv[:, :HW].astype(BF16) * jnp.asarray(DH ** -0.5, BF16)
            k_ref[...] = qkv[:, HW:2 * HW].astype(BF16)
            v_ref[...] = qkv[:, 2 * HW:].astype(BF16)
            kt_ref[...] = jnp.transpose(qkv[:, HW:2 * HW]).astype(BF16)
            vt_ref[...] = jnp.transpose(qkv[:, 2 * HW:]).astype(BF16)


def by_head(rows, heads):
    lane = lax.broadcasted_iota(jnp.int32, rows.shape, 1)
    zero = jnp.zeros_like(rows)
    return jnp.concatenate(
        [jnp.where((lane >= h * DH) & (lane < (h + 1) * DH), rows, zero) for h in range(heads)], axis=0
    )


def seg_at(index):
    if isinstance(index, int):
        return slice(index * SEG, (index + 1) * SEG)
    return pl.ds(pl.multiple_of(index * SEG, SEG), SEG)


def head_columns(acc, heads):
    pieces = [acc[h * DH:(h + 1) * DH, h * SEG:(h + 1) * SEG] for h in range(heads)]
    pieces.append(jnp.zeros((HW - heads * DH, SEG), F32))
    return jnp.concatenate(pieces, axis=0)


def pair_bias(bias_ref, first, second):
    return jnp.concatenate([bias_ref[first], bias_ref[second]], axis=1)


def attn_forward_kernel(
    heads, me_ref, parent_ref, q_ref, k_ref, v_ref, vt_ref, bias_ref, o0, o1, o2, o3, raw_ref, lse_ref, out_all
):
    cols = heads * SEG
    trunk_len = TRUNK * SEG
    last = trunk_len - SEG

    def queries(b):
        return by_head(q_ref[seg_at(b), :], heads)

    def finish(b, acc, total, top):
        lse_ref[pl.ds(b * 8, 8), :] = jnp.broadcast_to(top + jnp.log(total), (8, cols))
        columns = head_columns(acc / total, heads)
        raw_ref[:, seg_at(b)] = columns
        out_all[:, seg_at(b)] = columns.astype(BF16)

    for j in range(TRUNK // 2):
        q6 = jnp.concatenate([queries(2 * j), queries(2 * j + 1)], axis=0)
        scores = dot(k_ref[0:(j + 1) * 2 * SEG, :], q6, NT)
        parts = []
        if j > 0:
            far = (2 * j - 1) * SEG
            parts = [scores[:far], scores[far:far + SEG] + pair_bias(bias_ref, 1, 0)]
        parts.append(scores[2 * j * SEG:(2 * j + 1) * SEG] + pair_bias(bias_ref, 2, 1))
        parts.append(scores[(2 * j + 1) * SEG:] + pair_bias(bias_ref, 3, 2))
        top = functools.reduce(jnp.maximum, [jnp.max(part, axis=0, keepdims=True) for part in parts])
        parts = [jnp.exp(part - top) for part in parts]
        total = functools.reduce(jnp.add, [jnp.sum(part, axis=0, keepdims=True) for part in parts])
        acc = dot(vt_ref[:, 0:(j + 1) * 2 * SEG], jnp.concatenate([p.astype(BF16) for p in parts], axis=0), NN)
        for s in range(2):
            at = slice(s * cols, (s + 1) * cols)
            finish(2 * j + s, acc[:, at], total[:, at], top[:, at])

    def other_step(i, carry):
        segs = [TRUNK + 2 * i, TRUNK + 2 * i + 1]
        parents = [parent_ref[b] for b in segs]
        leaf = [(parent >= TRUNK).astype(jnp.int32) for parent in parents]
        q3 = [queries(b) for b in segs]
        q6 = jnp.concatenate(q3, axis=0)
        scores = dot(k_ref[0:trunk_len, :], q6, NT)
        near = scores[last:] + pair_bias(bias_ref, 1 - leaf[0], 1 - leaf[1])
        far = scores[:last]
        extra = []
        for s in range(2):
            keys = jnp.concatenate([k_ref[seg_at(parents[s]), :], k_ref[seg_at(segs[s]), :]], axis=0)
            bias = jnp.concatenate([bias_ref[3 - 2 * leaf[s]], bias_ref[2]], axis=0)
            extra.append(dot(keys, q3[s], NT) + bias)
        top = jnp.maximum(jnp.max(far, axis=0, keepdims=True), jnp.max(near, axis=0, keepdims=True))
        top = jnp.maximum(top, jnp.concatenate([jnp.max(e, axis=0, keepdims=True) for e in extra], axis=1))
        far, near = jnp.exp(far - top), jnp.exp(near - top)
        extra = [jnp.exp(extra[s] - top[:, s * cols:(s + 1) * cols]) for s in range(2)]
        total = jnp.sum(far, axis=0, keepdims=True) + jnp.sum(near, axis=0, keepdims=True)
        total = total + jnp.concatenate([jnp.sum(e, axis=0, keepdims=True) for e in extra], axis=1)
        acc = dot(vt_ref[:, 0:trunk_len], jnp.concatenate([far.astype(BF16), near.astype(BF16)], axis=0), NN)
        for s in range(2):
            at = slice(s * cols, (s + 1) * cols)
            values = jnp.concatenate([vt_ref[:, seg_at(parents[s])], vt_ref[:, seg_at(segs[s])]], axis=1)
            finish(segs[s], acc[:, at] + dot(values, extra[s].astype(BF16), NN), total[:, at], top[:, at])
        return carry

    lax.fori_loop(0, (SEGS - TRUNK) // 2, other_step, 0)
    for rel, o_ref in enumerate((o0, o1, o2, o3)):
        width, count = o_ref.shape
        at = pl.ds(pl.multiple_of(jnp.bitwise_xor(me_ref[0], rel) * count, SEG), count)
        o_ref[...] = out_all[0:width, at]


TRUNK_FIRST = [SEG * j * (j + 1) for j in range(TRUNK // 2 + 1)]
OTHER_ROWS = (TRUNK + 2) * SEG
PROB_ROWS = TRUNK_FIRST[-1] + (SEGS - TRUNK) // 2 * OTHER_ROWS


def attn_prob_kernel(heads, parent_ref, q_ref, k_ref, lse_ref, bias_ref, before_ref, out_ref):
    cols = heads * SEG

    def common(b):
        return by_head(q_ref[seg_at(b), :], heads), lse_ref[pl.ds(b * 8, 8), :][0:1]

    for j in range(TRUNK // 2):
        (qa, la), (qb, lb) = common(2 * j), common(2 * j + 1)
        q6, lse = jnp.concatenate([qa, qb], axis=0), jnp.concatenate([la, lb], axis=1)
        for i in range(j + 1):
            scores = dot(k_ref[2 * i * SEG:2 * (i + 1) * SEG, :], q6, NT)
            if i == j:
                scores = scores + jnp.concatenate([pair_bias(bias_ref, 2, 1), pair_bias(bias_ref, 3, 2)], axis=0)
            if i == j - 1:
                scores = scores + jnp.concatenate([pair_bias(bias_ref, 0, 0), pair_bias(bias_ref, 1, 0)], axis=0)
            first = TRUNK_FIRST[j] + 2 * i * SEG
            out_ref[first:first + 2 * SEG, :] = jnp.exp(scores - lse).astype(BF16)

    def other_step(step, carry):
        segs = [TRUNK + 2 * step, TRUNK + 2 * step + 1]
        parents = [parent_ref[b] for b in segs]
        leaf = [(parent >= TRUNK).astype(jnp.int32) for parent in parents]
        each = [common(b) for b in segs]
        q6, lse = jnp.concatenate([q for q, _ in each], axis=0), jnp.concatenate([l for _, l in each], axis=1)
        base = TRUNK_FIRST[-1] + step * OTHER_ROWS
        for i in range(TRUNK // 2):
            scores = dot(k_ref[2 * i * SEG:2 * (i + 1) * SEG, :], q6, NT)
            if i == TRUNK // 2 - 1:
                near = pair_bias(bias_ref, 1 - leaf[0], 1 - leaf[1])
                scores = scores + jnp.concatenate([jnp.zeros_like(near), near], axis=0)
            at = pl.ds(pl.multiple_of(base + 2 * i * SEG, SEG), 2 * SEG)
            out_ref[at, :] = jnp.exp(scores - lse).astype(BF16)
        extra = []
        for s in range(2):
            keys = jnp.concatenate([k_ref[seg_at(parents[s]), :], k_ref[seg_at(segs[s]), :]], axis=0)
            bias = jnp.concatenate([bias_ref[3 - 2 * leaf[s]], bias_ref[2]], axis=0)
            extra.append(jnp.exp(dot(keys, each[s][0], NT) + bias - each[s][1]).astype(BF16))
        at = pl.ds(pl.multiple_of(base + TRUNK * SEG, SEG), 2 * SEG)
        out_ref[at, :] = jnp.concatenate(extra, axis=1)
        return carry

    lax.fori_loop(0, (SEGS - TRUNK) // 2, other_step, 0)


def attn_backward_kernel(
    heads, me_ref, parent_ref, q_ref, k_ref, v_ref, kt_ref, raw_ref, prob_ref, g0, g1, g2, g3_ref,
    d0, d1, d2, d3, bins_ref, grad_all, dq_all, dk_acc, dv_acc, bins_acc, probs, sem,
):
    def fetch(step):
        if isinstance(step, int):
            at = pl.ds(TRUNK_FIRST[step], TRUNK_FIRST[step + 1] - TRUNK_FIRST[step])
        else:
            at = pl.ds(pl.multiple_of(TRUNK_FIRST[-1] + (step - TRUNK // 2) * OTHER_ROWS, SEG), OTHER_ROWS)
        return pltpu.make_async_copy(prob_ref.at[at, :], probs.at[at, :], sem.at[step])

    for j in range(TRUNK // 2):
        fetch(j).start()

    def start_other(step, carry):
        fetch(step + TRUNK // 2).start()
        return carry

    lax.fori_loop(0, (SEGS - TRUNK) // 2, start_other, 0)
    cols = heads * SEG
    trunk_len = TRUNK * SEG
    dk_acc[...] = jnp.zeros_like(dk_acc)
    dv_acc[...] = jnp.zeros_like(dv_acc)
    bins_acc[...] = jnp.zeros_like(bins_acc)
    for rel, g_ref in enumerate((g0, g1, g2, g3_ref)):
        width, count = g_ref.shape
        at = pl.ds(pl.multiple_of(jnp.bitwise_xor(me_ref[0], rel) * count, SEG), count)
        grad_all[0:width, at] = g_ref[...]
        grad_all[width:HW, at] = jnp.zeros((HW - width, count), BF16)

    def common(b):
        q3 = by_head(q_ref[seg_at(b), :], heads)
        grad = grad_all[:, seg_at(b)].astype(F32)
        product = grad * raw_ref[:, seg_at(b)]
        row_dot = jnp.concatenate(
            [jnp.sum(product[h * DH:(h + 1) * DH], axis=0, keepdims=True) for h in range(heads)], axis=1
        )
        return q3, by_head(jnp.transpose(grad).astype(BF16), heads), row_dot

    def block(prob, values, g, row_dot):
        return prob.astype(F32) * (dot(values, g, NT) - row_dot)

    def write_dq(b, acc):
        dq_all[seg_at(b), :] = (jnp.transpose(head_columns(acc, heads)) * DH ** -0.5).astype(BF16)

    def both(pair):
        return [jnp.concatenate([a, b], axis=0 if a.shape[0] > 1 else 1) for a, b in zip(*pair)]

    for j in range(TRUNK // 2):
        q6, g6, row_dot = both([common(2 * j), common(2 * j + 1)])
        fetch(j).wait()
        kept = []
        for i in range(j + 1):
            at = slice(2 * i * SEG, 2 * (i + 1) * SEG)
            prob = probs[TRUNK_FIRST[j] + 2 * i * SEG:TRUNK_FIRST[j] + 2 * (i + 1) * SEG, :]
            score = block(prob, v_ref[at, :], g6, row_dot)
            if i == j:
                bins_acc[0] += score[:SEG, cols:]
                bins_acc[1] += score[:SEG, :cols] + score[SEG:, cols:]
            if i == j - 1:
                bins_acc[0] += score[SEG:, :cols]
            score = score.astype(BF16)
            dv_acc[at, :] += dot(prob, g6, NN)
            dk_acc[at, :] += dot(score, q6, NN)
            kept.append(score)
        acc = dot(kt_ref[:, 0:(j + 1) * 2 * SEG], jnp.concatenate(kept, axis=0), NN)
        for s in range(2):
            write_dq(2 * j + s, acc[:, s * cols:(s + 1) * cols])

    def other_step(step, carry):
        segs = [TRUNK + 2 * step, TRUNK + 2 * step + 1]
        parents = [parent_ref[b] for b in segs]
        leaf = [(parent >= TRUNK).astype(jnp.int32) for parent in parents]
        each = [common(b) for b in segs]
        q6, g6, row_dot = both(each)
        base = TRUNK_FIRST[-1] + step * OTHER_ROWS
        fetch(step + TRUNK // 2).wait()
        kept = []
        for i in range(TRUNK // 2):
            at = slice(2 * i * SEG, 2 * (i + 1) * SEG)
            prob = probs[pl.ds(pl.multiple_of(base + 2 * i * SEG, SEG), 2 * SEG), :]
            score = block(prob, v_ref[at, :], g6, row_dot)
            if i == TRUNK // 2 - 1:
                for s in range(2):
                    bins_acc[0] += jnp.where(leaf[s] == 0, score[SEG:, s * cols:(s + 1) * cols], 0.0)
            score = score.astype(BF16)
            dv_acc[at, :] += dot(prob, g6, NN)
            dk_acc[at, :] += dot(score, q6, NN)
            kept.append(score)
        acc = dot(kt_ref[:, 0:trunk_len], jnp.concatenate(kept, axis=0), NN)
        for s in range(2):
            q3, g3, row = each[s]
            first, second = seg_at(parents[s]), seg_at(segs[s])
            values = jnp.concatenate([v_ref[first, :], v_ref[second, :]], axis=0)
            keys_t = jnp.concatenate([kt_ref[:, first], kt_ref[:, second]], axis=1)
            at = pl.ds(pl.multiple_of(base + trunk_len, SEG), 2 * SEG)
            prob = probs[at, s * cols:(s + 1) * cols]
            score = block(prob, values, g3, row)
            bins_acc[0] += score[:SEG]
            bins_acc[1] += score[SEG:]
            score = score.astype(BF16)
            grad_v, grad_k = dot(prob, g3, NN), dot(score, q3, NN)
            dv_acc[first, :] += grad_v[:SEG]
            dv_acc[second, :] += grad_v[SEG:]
            dk_acc[first, :] += grad_k[:SEG]
            dk_acc[second, :] += grad_k[SEG:]
            write_dq(segs[s], acc[:, s * cols:(s + 1) * cols] + dot(keys_t, score, NN))
        return carry

    lax.fori_loop(0, (SEGS - TRUNK) // 2, other_step, 0)
    for rel, d_ref in enumerate((d0, d1, d2, d3)):
        count = d_ref.shape[0]
        width = heads * DH
        at = pl.ds(pl.multiple_of(jnp.bitwise_xor(me_ref[0], rel) * count, SEG), count)
        parts = [dq_all[at, :][:, :width], dk_acc[at, :][:, :width].astype(BF16), dv_acc[at, :][:, :width].astype(BF16)]
        parts.append(jnp.zeros((count, d_ref.shape[1] - 3 * width), BF16))
        d_ref[...] = jnp.concatenate(parts, axis=1)
    key = lax.broadcasted_iota(jnp.int32, (SEG, cols), 0)
    query = lax.broadcasted_iota(jnp.int32, (SEG, cols), 1) % SEG
    gap = query - key
    parent_sum, own_sum = bins_acc[0], bins_acc[1]
    lines = [jnp.sum(parent_sum + own_sum, axis=0, keepdims=True)]
    for threshold in THRESHOLDS:
        hit = jnp.where(gap + SEG >= threshold, parent_sum, 0.0) + jnp.where(gap >= threshold, own_sum, 0.0)
        lines.append(jnp.sum(hit, axis=0, keepdims=True))
    bins_ref[...] = jnp.concatenate(lines, axis=0)


class Slots:
    def __init__(self, n_expert, capacity):
        self.n_expert = n_expert
        self.cut = n_expert == 8
        self.block = -(-(capacity + SPARE) // 16) * 16
        if self.cut:
            self.groups = [[0, 1, 4, 5], [2, 3, 6, 7]]
            self.rels = [2, 3, 6, 7]
            self.chunks = [[[0, 1, 2, 3]], [[4], [5], [6], [7]]]
        else:
            self.groups = None
            self.chunks = [[list(range(n_expert))]]
        self.arrays = [array for chunk in self.chunks for array in chunk]

    def block_of(self, expert, me):
        if not self.cut:
            return expert
        rel = jnp.bitwise_xor(expert, me)
        inside = lambda index: (index & 1) | ((index >> 1) & 2)
        return jnp.where((rel & 2) == 0, inside(expert), 4 + inside(rel))

    def expert_of(self, block, me):
        if not self.cut:
            return block
        if not isinstance(block, int) or block < 4:
            return (me & 2) | (block & 1) | ((block & 2) << 1)
        return jnp.bitwise_xor(me, self.rels[block - 4])

    def near_exchange(self, block):
        return lax.all_to_all(block, "expert", split_axis=0, concat_axis=0, tiled=True, axis_index_groups=self.groups)


def over_experts(block):
    return lax.all_to_all(block, "expert", split_axis=0, concat_axis=0, tiled=True)


def swap(block, axis, rel):
    if rel == 0:
        return block
    return lax.ppermute(block, axis, [(i, i ^ rel) for i in range(lax.axis_size(axis))])


def swap_all(blocks, axis):
    return [swap(block, axis, rel) for rel, block in enumerate(blocks)]


def from_all(block):
    near, far = swap(block, "shard", 1), swap(block, "shard", 2)
    return [block, near, far, swap(far, "shard", 1)]


def reorder(parts, me):
    bit = 1
    while bit < len(parts):
        parts = [jnp.where(me & bit, parts[i ^ bit], parts[i]) for i in range(len(parts))]
        bit *= 2
    return parts


def send_rows(slots, rows, places_ref, out_refs):
    tokens = places_ref.shape[1]
    for array, out_ref in zip(slots.arrays, out_refs):
        for i, block in enumerate(array):
            slot = block * slots.block + lax.broadcasted_iota(jnp.int32, (slots.block, tokens), 0)
            hit = (slot == places_ref[0:1, :]) | (slot == places_ref[1:2, :])
            picked = dot(jnp.where(hit, 1.0, 0.0).astype(BF16), rows, NN).astype(BF16)
            out_ref[i * slots.block:(i + 1) * slots.block, :] = picked


def row_at(first, count):
    return pl.ds(first if isinstance(first, int) else pl.multiple_of(first, 16), count)


def diagonal(count):
    return lax.broadcasted_iota(jnp.int32, (count, count), 0) == lax.broadcasted_iota(jnp.int32, (count, count), 1)


def padded_row(row, width):
    count = row.shape[1]
    return row if count == width else jnp.concatenate([row, jnp.zeros((1, width - count), row.dtype)], axis=1)


def dispatch_kernel(slots, me_ref, places_ref, others_ref, rows_ref, *refs):
    out_ref = refs[-1]
    tokens = places_ref.shape[1]
    width = rows_ref.shape[1]
    rows = rows_ref[...]
    count = slots.block

    def one(expert, carry):
        slot = slots.block_of(expert, me_ref[0]) * count + lax.broadcasted_iota(jnp.int32, (count, tokens), 0)
        hot = [jnp.where(slot == places_ref[j:j + 1, :], 1.0, 0.0).astype(BF16) for j in range(2)]
        picked = dot(hot[0] + hot[1], rows, NN)
        ids = sum(dot(others_ref[8 * j:8 * j + 8, :], hot[j], NT) for j in range(2))
        line = lax.broadcasted_iota(jnp.int32, picked.shape, 0)
        picked = jnp.where(line == count - 1, padded_row(ids[0:1], width), picked)
        out_ref[pl.ds(pl.multiple_of(expert * count, 16), count), :] = picked.astype(BF16)
        return carry

    lax.fori_loop(0, slots.n_expert, one, 0)


def post_kernel(
    slots, me_ref, x_ref, gain_ref, router_ref, routes_ref, places_ref, m0, m1, m2, m3, w_ref,
    after_ref, normed_ref, gates_ref, *out_refs,
):
    after = x_ref[...].astype(F32)
    for rel, m_ref in enumerate((m0, m1, m2, m3)):
        after = after + dot(m_ref[...], w_ref[jnp.bitwise_xor(me_ref[1], rel)], TN)
    after_ref[...] = after
    unit, _ = rms_parts(after)
    normed = (unit * gain_ref[...]).astype(BF16)
    normed_ref[...] = normed
    send_rows(slots, normed_ref[...], places_ref, out_refs)
    logits = dot(normed, router_ref[...], NN)
    expert = lax.broadcasted_iota(jnp.int32, logits.shape, 1)
    first = jnp.sum(jnp.where(expert == routes_ref[:, 0:1], logits, 0.0), axis=-1, keepdims=True)
    second = jnp.sum(jnp.where(expert == routes_ref[:, 1:2], logits, 0.0), axis=-1, keepdims=True)
    top = jnp.maximum(first, second)
    first, second = jnp.exp(first - top), jnp.exp(second - top)
    gates_ref[...] = jnp.concatenate([first / (first + second), second / (first + second)], axis=1)


def expert_kernel(slots, kind, sizes, before, me_ref, *refs):
    refs = list(refs)
    take = lambda n: [refs.pop(0) for _ in range(n)]
    x_refs = take(sizes[0])
    g_all, router_ref = take(2)
    first_refs, second_refs = take(4), take(4)
    extra = take(before)
    own_ref = extra[1] if before == 3 else None
    (out_all,) = take(1)
    dx_refs = take(sizes[1])
    rows_ref, grad_ref, act_ref, inner_ref, first_buf, second_buf, g_buf, out_buf, out_acc, dx_acc, gate_acc, gates_acc, sem, in_sem = refs
    step = pl.program_id(0)
    slot = lax.rem(step, 2)
    total, width = rows_ref.shape
    depth, units = first_refs[0].shape[0], second_buf.shape[1]

    def fetch(rel, slot):
        column = pl.multiple_of(jnp.bitwise_xor(me_ref[1], rel) * units, 128)
        copies = [pltpu.make_async_copy(second_refs[rel], second_buf.at[slot], in_sem.at[slot, 4])]
        for piece, ref in enumerate(first_refs):
            row = pl.multiple_of(jnp.bitwise_xor(me_ref[1], piece) * depth, 16)
            copies.append(
                pltpu.make_async_copy(
                    ref.at[:, pl.ds(column, units)], first_buf.at[slot, pl.ds(row, depth), :], in_sem.at[slot, piece]
                )
            )
        return copies

    @pl.when(step == 0)
    def _():
        for copy in fetch(0, 0):
            copy.start()

    for rel in range(4):
        @pl.when(step == rel)
        def _(rel=rel):
            if rel < 3:
                for copy in fetch(rel + 1, (rel + 1) % 2):
                    copy.start()
    rows = slots.block
    mine = slots.block_of(me_ref[0], me_ref[0])
    if kind == "own":
        pieces = [(mine, x_refs[0], mine * rows, dx_refs[0], 0)]
    elif kind == "near":
        blocks = [jnp.bitwise_xor(mine, i) for i in (1, 2, 3)]
        pieces = [(block, x_refs[0], block * rows, dx_refs[0], block * rows) for block in blocks]
    elif kind == "far":
        pieces = [(4 + i, x_ref, 0, dx_ref, 0) for i, (x_ref, dx_ref) in enumerate(zip(x_refs, dx_refs))]
    else:
        pieces = [(block, x_refs[0], block * rows, dx_refs[0], block * rows) for block in range(slots.n_expert)]
    pieces = [(*piece, i * rows) for i, piece in enumerate(pieces)]

    def home(block):
        return pl.ds(pl.multiple_of(slots.expert_of(block, me_ref[0]) * rows, 16), rows)

    @pl.when(step == 0)
    def _():
        copies = [
            pltpu.make_async_copy(g_all.at[home(block), :], g_buf.at[pl.ds(first, rows), :], sem.at[i])
            for i, (block, *_, first) in enumerate(pieces)
        ]
        for copy in copies:
            copy.start()
        out_acc[...] = jnp.zeros_like(out_acc)
        dx_acc[...] = jnp.zeros_like(dx_acc)
        for _, x_ref, inside, _, _, first in pieces:
            rows_ref[first:first + rows, :] = x_ref[row_at(inside, rows), :]
        for copy in copies:
            copy.wait()
        for *_, first in pieces:
            at = slice(first, first + rows)
            grads = g_buf[at, :].astype(F32)
            other = jnp.sum(jnp.where(diagonal(rows), grads[rows - 1:, :rows], 0.0), axis=1, keepdims=True).astype(jnp.int32)
            logits = dot(rows_ref[at, :], router_ref[...], NN)
            expert = lax.broadcasted_iota(jnp.int32, logits.shape, 1)
            mine = jnp.sum(jnp.where(expert == me_ref[0], logits, 0.0), axis=-1, keepdims=True)
            its = jnp.sum(jnp.where(expert == other, logits, 0.0), axis=-1, keepdims=True)
            top = jnp.maximum(mine, its)
            mine, its = jnp.exp(mine - top), jnp.exp(its - top)
            line = lax.broadcasted_iota(jnp.int32, grads.shape, 0)
            gate = mine / (mine + its)
            gate_acc[at, :] = jnp.broadcast_to(gate, (rows, 128))
            grad_ref[at, :] = jnp.where(line < rows - SPARE, gate * grads, 0.0).astype(BF16)

    for rel in range(4):
        @pl.when(step == rel)
        def _(rel=rel):
            for copy in fetch(rel, rel % 2):
                copy.wait()

    parts = 1
    while total // parts > 512 or total % parts or (total // parts) % 16:
        parts += 1
    part = total // parts
    for i in range(parts):
        at = slice(i * part, (i + 1) * part)
        first_w, second_w = first_buf[slot], second_buf[slot]
        value = dot(rows_ref[at, :], first_w, NN)
        grad_act = dot(grad_ref[at, :], second_w, NT)
        square = value * value
        half = 0.5 * value
        scale = 0.7978845608028654
        th = jnp.tanh(value * (scale + (scale * 0.044715) * square))
        act = (half + half * th).astype(BF16)
        slope = 0.5 + 0.5 * th + (half * (1.0 - th * th)) * (scale + (3 * scale * 0.044715) * square)
        inner = (grad_act * slope).astype(BF16)
        act_ref[at, :] = act
        inner_ref[at, :] = inner
        out_acc[at, :] += dot(act, second_w, NN)
        dx_acc[at, :] += dot(inner, first_w, NT)

    @pl.when(step == pl.num_programs(0) - 1)
    def _():
        for *_, first in pieces:
            at = slice(first, first + rows)
            out = out_acc[at, :].astype(BF16).astype(F32)
            gates = jnp.sum(out * g_buf[at, :].astype(F32), axis=1, keepdims=True)
            gates_acc[at, :] = jnp.broadcast_to(gates, (rows, 128))
            out_buf[at, :] = (gate_acc[at, 0:1] * out).astype(BF16)
        copies = [
            pltpu.make_async_copy(out_buf.at[pl.ds(first, rows), :], out_all.at[home(block), :], sem.at[i])
            for i, (block, *_, first) in enumerate(pieces)
        ]
        for copy in copies:
            copy.start()
        if own_ref is not None:
            dx_refs[0][row_at(mine * rows, rows), :] = own_ref[...]
        for _, _, _, dx_ref, inside, first in pieces:
            at = slice(first, first + rows)
            gates = gates_acc[at, 0:1]
            gates = jnp.sum(jnp.where(diagonal(rows), gates, 0.0), axis=0, keepdims=True)
            dx_ref[row_at(inside, rows), :] = dx_acc[at, :].astype(BF16)
            tail = dx_acc[first + rows - 16:first + rows, :]
            line = lax.broadcasted_iota(jnp.int32, tail.shape, 0)
            for place in range(SPARE):
                piece = gates.astype(BF16).astype(F32)
                gates = gates - piece
                tail = jnp.where(line == 16 - SPARE + place, padded_row(piece, width), tail)
            dx_ref[row_at(inside + rows - 16, 16), :] = tail.astype(BF16)
        for copy in copies:
            copy.wait()


def run_expert(slots, kind, blocks, dx_shape, shared, before, estimate):
    me, g_all, router, first_w, second_w = shared
    hidden, width = first_w[0].shape[1], router.shape[0]
    total = slots.block * {"own": 1, "near": 3, "far": 4, "all": slots.n_expert}[kind]
    block = hidden // 4
    whole = lambda a: pl.BlockSpec(a.shape, lambda i: (0, 0))
    column = pl.BlockSpec((total, block), lambda i: (0, i))
    rows = pl.BlockSpec((total, width), lambda i: (0, 0))
    fresh = len(before) < 2
    dx = [jax.ShapeDtypeStruct(dx_shape, BF16)] * (4 if kind == "far" else 1)
    inputs = [me, *blocks, g_all, router, *first_w, *second_w, *before]
    before_specs = [ANY] * len(before)
    if len(before) == 3:
        before_specs[1] = whole(before[1])
    return pl.pallas_call(
        functools.partial(expert_kernel, slots, kind, (len(blocks), len(dx)), len(before)),
        grid=(4,),
        in_specs=[SMEM] + [whole(b) for b in blocks] + [ANY, whole(router)] + [ANY] * 8 + before_specs,
        out_specs=[ANY] + [whole(b) for b in dx] + [rows, rows, column, column],
        out_shape=arrays(
            (g_all.shape, BF16), *[(b.shape, BF16) for b in dx], *[((total, width), BF16)] * 2, *[((total, hidden), BF16)] * 2
        ),
        scratch_shapes=[
            pltpu.VMEM((2, width, block), BF16),
            pltpu.VMEM((2, block, width), BF16),
            pltpu.VMEM((total, width), BF16),
            pltpu.VMEM((total, width), BF16),
            pltpu.VMEM((total, width), F32),
            pltpu.VMEM((total, width), F32),
            pltpu.VMEM((total, 128), F32),
            pltpu.VMEM((total, 128), F32),
            pltpu.SemaphoreType.DMA((total // slots.block,)),
            pltpu.SemaphoreType.DMA((2, 5)),
        ],
        input_output_aliases={} if fresh else {len(inputs) - 1: 0},
        compiler_params=params(dimension_semantics=("arbitrary",)),
        cost_estimate=estimate,
    )(*inputs)


def first_grad_kernel(parts, me_ref, *refs):
    send_ref, keep_ref, total = refs[-3:]
    total[...] = sum(dot(x[...], inner[...], TN) for x, inner in zip(refs[:parts], refs[parts:2 * parts]))
    depth = send_ref.shape[0] // 2
    for rel in range(4):
        ref = (keep_ref, send_ref)[rel % 2]
        row = pl.multiple_of(jnp.bitwise_xor(me_ref[1], rel) * depth, 16)
        at = rel // 2 * depth
        ref[at:at + depth, :] = total[pl.ds(row, depth), :].astype(BF16)


def run_first_grad(me, rows, inners, depth, *after):
    width, hidden = rows[0].shape[1], inners[0].shape[1]
    block = hidden // 4
    column = pl.BlockSpec((2 * depth, block), lambda i, me_ref: (0, jnp.bitwise_xor(me_ref[1], i)))
    return pl.pallas_call(
        functools.partial(first_grad_kernel, len(rows)),
        grid_spec=pltpu.PrefetchScalarGridSpec(
            num_scalar_prefetch=1,
            grid=(4,),
            in_specs=[pl.BlockSpec(a.shape, lambda i, me_ref: (0, 0)) for a in rows]
            + [pl.BlockSpec((a.shape[0], block), lambda i, me_ref: (0, i)) for a in inners]
            + [ANY] * len(after),
            out_specs=[column, column],
            scratch_shapes=[pltpu.VMEM((width, block), F32)],
        ),
        out_shape=arrays(*[((2 * depth, hidden), BF16)] * 2),
        compiler_params=params(dimension_semantics=("arbitrary",)),
        cost_estimate=SHORT,
    )(me, *rows, *inners, *after)


def second_grad_kernel(parts, *refs):
    send_ref, keep_ref = refs[2 * parts:]
    step = pl.program_id(0)
    block = sum(dot(act[...], g[...], TN) for act, g in zip(refs[:parts], refs[parts:2 * parts])).astype(BF16)

    @pl.when(step < 2)
    def _():
        send_ref[...] = block

    @pl.when(step >= 2)
    def _():
        keep_ref[...] = block


def run_second_grad(acts, grads):
    width, hidden = grads[0].shape[1], acts[0].shape[1]
    block = hidden // 4
    return pl.pallas_call(
        functools.partial(second_grad_kernel, len(acts)),
        grid=(4,),
        in_specs=[pl.BlockSpec((a.shape[0], block), lambda i: (0, 2 * (i % 2) + 1 - i // 2)) for a in acts]
        + [pl.BlockSpec(a.shape, lambda i: (0, 0)) for a in grads],
        out_specs=[
            pl.BlockSpec((block, width), lambda i: (jnp.minimum(i, 1), 0)),
            pl.BlockSpec((block, width), lambda i: (jnp.maximum(i - 2, 0), 0)),
        ],
        out_shape=arrays(*[((2 * block, width), BF16)] * 2),
        compiler_params=params(dimension_semantics=("arbitrary",)),
        cost_estimate=SHORT,
    )(*acts, *grads)


def core_sum(send, keep):
    near = swap(send, "shard", 1)
    half = keep.shape[0] // 2
    other = (keep[half:].astype(F32) + near[half:].astype(F32)).astype(BF16)
    return keep, near, other


def across_sum(parts):
    keep, near, other = parts
    return keep, near, swap(other, "shard", 2)


def total_sum(parts):
    keep, near, far = parts
    half = keep.shape[0] // 2
    return keep[:half].astype(F32) + near[:half].astype(F32) + far.astype(F32)


def gather_blocks(slots, refs, scratch):
    for array, ref in zip(slots.arrays, refs):
        scratch[array[0] * slots.block:(array[-1] + 1) * slots.block, :] = ref[...]


def back_kernel(slots, me_ref, *refs):
    refs_left = list(refs)
    take = lambda n: [refs_left.pop(0) for _ in range(n)]
    ret_refs = take(len(slots.arrays))
    places_ref, routes_ref, gates_ref, after_ref, gain_ref, router_ref, g_ref = take(7)
    w_ref, normed_ref = take(2)
    m_refs = take(4)
    (grad_after_ref,) = take(1)
    mixed_refs = take(4)
    send_ref, keep_ref, branch_ref, glogits_ref, ggain_ref, more, scratch = refs_left
    tokens = after_ref.shape[0]
    part = tokens // 2
    gather_blocks(slots, ret_refs, scratch)
    pieces = []
    for end in range(slots.block, scratch.shape[0] + 1, slots.block):
        tail = scratch[end - 16:end, :].astype(F32)[16 - SPARE:, :slots.block]
        pieces.append(jnp.sum(tail, axis=0, keepdims=True))
    gg = jnp.concatenate(pieces, axis=1)
    ggain_ref[...] = jnp.zeros_like(ggain_ref)

    def one(i, carry):
        at = pl.ds(pl.multiple_of(i * part, part), part)
        slot = lax.broadcasted_iota(jnp.int32, (part, gg.shape[1]), 1)
        hit0, hit1 = slot == places_ref[at, 0:1], slot == places_ref[at, 1:2]
        gg0 = jnp.sum(jnp.where(hit0, gg, 0.0), axis=-1, keepdims=True)
        gg1 = jnp.sum(jnp.where(hit1, gg, 0.0), axis=-1, keepdims=True)
        total = dot(jnp.where(hit0 | hit1, 1.0, 0.0).astype(BF16), scratch[...], NN)
        gate0, gate1 = gates_ref[at, 0:1], gates_ref[at, 1:2]
        mean = gate0 * gg0 + gate1 * gg1
        expert = lax.broadcasted_iota(jnp.int32, (part, router_ref.shape[1]), 1)
        glogits = jnp.where(expert == routes_ref[at, 0:1], gate0 * (gg0 - mean), 0.0) + jnp.where(
            expert == routes_ref[at, 1:2], gate1 * (gg1 - mean), 0.0
        )
        glogits = glogits.astype(BF16)
        glogits_ref[at, :] = glogits
        incoming = dot(glogits, router_ref[...], NT) + total
        unit, factor = rms_parts(after_ref[at, :])
        grad_after = g_ref[at, :].astype(F32) + rms_grad(incoming, gain_ref[...], unit, factor)
        ggain_ref[0:1, :] += jnp.sum(incoming * unit, axis=0, keepdims=True)
        grad_after_ref[at, :] = grad_after
        branch = grad_after.astype(BF16)
        branch_ref[at, :] = branch
        return carry

    lax.fori_loop(0, tokens // part, one, 0)
    for rel, mixed_ref in enumerate(mixed_refs):
        mixed_ref[...] = dot(w_ref[jnp.bitwise_xor(me_ref[0], rel)], branch_ref[...], NT).astype(BF16)
    width = branch_ref.shape[1]
    grad_router = dot(normed_ref[...], glogits_ref[...], TN)
    gain = jnp.transpose(jnp.concatenate([ggain_ref[...]] * 16, axis=0))[:, 0:1]
    blank = jnp.zeros((width, more.shape[1] - grad_router.shape[1] - 1), F32)
    more[...] = jnp.concatenate([grad_router, gain, blank], axis=1)
    for rel, m_ref in enumerate(m_refs):
        ref = (keep_ref, send_ref)[rel % 2]
        count = m_ref.shape[0]
        at = slice(rel // 2 * count, (rel // 2 + 1) * count)
        ref[at, 0:width] = dot(m_ref[...], branch_ref[...], NN).astype(BF16)
        row = pl.multiple_of(jnp.bitwise_xor(me_ref[0], rel) * count, 16)
        ref[at, width:] = more[pl.ds(row, count), :].astype(BF16)


def combine_kernel(slots, me_ref, ret_ref, places_ref, after_ref, out_ref, scratch):
    part = after_ref.shape[0] // 2
    for block in range(slots.n_expert):
        first = pl.multiple_of(slots.expert_of(block, me_ref[0]) * slots.block, 16)
        scratch[block * slots.block:(block + 1) * slots.block, :] = ret_ref[pl.ds(first, slots.block), :]

    def one(i, carry):
        at = pl.ds(pl.multiple_of(i * part, part), part)
        slot = lax.broadcasted_iota(jnp.int32, (part, scratch.shape[0]), 1)
        hit = (slot == places_ref[at, 0:1]) | (slot == places_ref[at, 1:2])
        total = after_ref[at, :] + dot(jnp.where(hit, 1.0, 0.0).astype(BF16), scratch[...], NN)
        out_ref[at, :] = total.astype(BF16)
        return carry

    lax.fori_loop(0, after_ref.shape[0] // part, one, 0)


def final_kernel(me_ref, x_ref, gain_ref, after_ref, d0, d1, d2, d3, w_ref, out_ref):
    grad = sum(
        dot(d_ref[...], w_ref[jnp.bitwise_xor(me_ref[0], rel)], NT) for rel, d_ref in enumerate((d0, d1, d2, d3))
    )
    unit, factor = rms_parts(x_ref[...].astype(F32))
    out_ref[...] = (after_ref[...] + rms_grad(grad, gain_ref[...], unit, factor)).astype(BF16)


def column_grad_kernel(
    orders, heads, me_ref, bins_ref, n_ref, d0, d1, d2, d3, wk_ref, wn_ref, wf_ref, *refs
):
    *out_refs, acc, more = refs
    acc[...] = sum(dot(n_ref[rel], d_ref[...], TN) for rel, d_ref in enumerate((d0, d1, d2, d3)))
    rows = wf_ref.shape[0]
    more[...] = wk_ref[0:rows, :].astype(F32) + wn_ref[0:rows, :].astype(F32) + wf_ref[...].astype(F32)
    cols = 3 * heads * DH
    wide = acc.shape[1]
    lane = lax.broadcasted_iota(jnp.int32, (NB, wide), 1)
    table = jnp.zeros((NB, wide), F32)
    for h in range(heads):
        above = jnp.sum(bins_ref[:, h * SEG:(h + 1) * SEG], axis=1, keepdims=True)
        column = above - jnp.concatenate([above[1:], jnp.zeros((1, 1), F32)], axis=0)
        column = jnp.concatenate([column[:-1], -jnp.sum(column[:-1], axis=0, keepdims=True)], axis=0)
        table = jnp.where(lane == cols + h, column, table)
    share = rows // len(orders[0])
    half = share // 2

    def block_of(rel):
        first = jnp.bitwise_xor(me_ref[0], rel) * share
        at = lambda start: pl.ds(pl.multiple_of(start + first, 8), share)
        block = [acc[at(p * rows), :] for p in range(4)]
        block[0] = jnp.concatenate([block[0][:NB] + table, block[0][NB:]], axis=0)
        others = more[at(0), :]
        rest = others[:, wide:]
        folded = [rest[:half], rest[half:], jnp.zeros((half, wide - 2 * rest.shape[1]), F32)]
        block += [others[:, :wide], jnp.concatenate(folded, axis=1)]
        if half % 8:
            block.append(jnp.zeros((-half % 8, wide), F32))
        return block[:3], block[3:]

    blocks = {rel: block_of(rel) for rel in orders[0]}
    count = len(out_refs) // 2
    for part, order in enumerate(orders):
        for i in range(count):
            mine = order[i * len(order) // count:(i + 1) * len(order) // count]
            rows_of = [row for rel in mine for row in blocks[rel][part]]
            out_refs[part * count + i][...] = jnp.concatenate(rows_of, axis=0).astype(BF16)


def split_kernel(me_ref, *refs):
    *in_refs, b0, b1, b2, b3, more_ref, table_ref, total = refs
    share, cols = b0.shape
    count = len(in_refs) // 2
    total[0:3 * share, :] = sum(ref[...].astype(F32) for ref in in_refs[:count])
    total[3 * share:, :] = sum(ref[...].astype(F32) for ref in in_refs[count:])
    wide = total.shape[1]
    for rel, ref in enumerate((b0, b1, b2, b3)):
        at = pl.ds(pl.multiple_of(jnp.bitwise_xor(me_ref[0], rel) * share, 8), share)
        ref[...] = total[at, :][:, :cols].astype(BF16)
    folded = total[5 * share:5 * share + share // 2, :]
    rest = more_ref.shape[1] - wide
    folded = jnp.concatenate([folded[:, :rest], folded[:, rest:2 * rest]], axis=0)
    more_ref[...] = jnp.concatenate([total[4 * share:5 * share, :], folded], axis=1).astype(BF16)
    table_ref[...] = total[0:NB, wide - table_ref.shape[1]:]


def join_kernel(me_ref, p0, p1, p2, p3, more_ref, out_ref):
    parts = [ref[...] for ref in (p0, p1, p2, p3)]
    for bit in (1, 2):
        swapped = (me_ref[0] & bit) != 0
        parts = [jnp.where(swapped, parts[i ^ bit], parts[i]) for i in range(4)]
    hw = p0.shape[1] // 3
    out_ref[...] = jnp.concatenate(
        [part[:, c * hw:(c + 1) * hw] for c in range(3) for part in parts] + [more_ref[...]], axis=1
    )


def place_kernel(experts, me_ref, wq_ref, wk_ref, wv_ref, gain_in_ref, *refs):
    *piece_refs, q_ref, k_ref, v_ref, o_ref, router_ref, gains_ref, more = refs
    width = q_ref.shape[1]
    count = piece_refs[0].shape[0] // (2 if len(piece_refs) > 1 else 1)
    for rel, at_row, piece_ref in [
        (rel | (first // count) * 4, first, ref) for rel, ref in enumerate(piece_refs) for first in range(0, ref.shape[0], count)
    ]:
        at = pl.ds(pl.multiple_of(jnp.bitwise_xor(me_ref[0], rel) * count, 8), count)
        piece = piece_ref[at_row:at_row + count, :].astype(F32)
        for c, out_ref in enumerate((q_ref, k_ref, v_ref, o_ref)):
            out_ref[at, :] = piece[:, c * width:(c + 1) * width]
        more[at, :] = piece[:, 4 * width:]
    total = sum(
        w_ref[...].astype(F32) * out_ref[...] for w_ref, out_ref in ((wq_ref, q_ref), (wk_ref, k_ref), (wv_ref, v_ref))
    )
    rows = total.shape[0]
    lane = lax.broadcasted_iota(jnp.int32, more.shape, 1)
    columns = jnp.where(lane == experts + 1, jnp.sum(total, axis=1, keepdims=True), more[...])
    columns = jnp.concatenate([columns, jnp.zeros((-rows % 128, columns.shape[1]), F32)], axis=0)
    columns = jnp.transpose(columns)[:, :rows]
    router_ref[...] = columns[0:experts]
    gains_ref[0:1, :] = columns[experts + 1:experts + 2] / gain_in_ref[...]
    gains_ref[1:2, :] = columns[experts:experts + 1]


def per_device(
    tokens, gain_attn, w_query, w_key, w_value, w_output, rel_table, gain_moe, router,
    w_in, w_out, routes, parents, cotangent,
):
    n_shard = lax.axis_size("shard")
    n_expert = lax.axis_size("expert")
    tok, width = tokens.shape
    tree_len = tok * n_shard
    n_experts = router.shape[1]
    heads = rel_table.shape[0]
    hw = heads * DH
    wide = -(-3 * hw // 128) * 128
    rows = width // n_shard
    slots = Slots(n_expert, max(2, tok * 20 // (7 * n_experts)))
    me_s, me_e = lax.axis_index("shard").astype(jnp.int32), lax.axis_index("expert").astype(jnp.int32)
    me_shard, me_expert, me = me_s.reshape(1), me_e.reshape(1), jnp.stack([me_e, me_s])

    more = jnp.concatenate([gain_attn[:, None], gain_moe[:, None], router], axis=1)
    w_rel = pl.pallas_call(
        columns_kernel,
        in_specs=[SMEM] + [VMEM] * 4,
        out_specs=[VMEM] * n_shard,
        out_shape=arrays(*[((rows, -(-(3 * hw + 2 + n_experts) // 128) * 128), BF16)] * n_shard),
        compiler_params=params(),
        cost_estimate=SHORT,
    )(me_shard, w_query, w_key, w_value, more)
    near_tokens, far_tokens = swap(tokens, "shard", 1), swap(tokens, "shard", 2)
    w_pieces = swap_all(w_rel, "shard")

    expert_range = jnp.arange(n_experts, dtype=jnp.int32)
    flat_routes = routes.reshape(-1)
    expert_hot = (flat_routes[:, None] == expert_range[None, :]).astype(jnp.int32)
    earlier = jnp.cumsum(expert_hot, axis=0) - expert_hot
    rank = jnp.sum(earlier * expert_hot, axis=-1)
    places = (slots.block_of(flat_routes, me_e) * slots.block + rank).reshape(tok, 2)
    places_row = places.T
    others = jnp.repeat(routes.T[::-1], 8, axis=0).astype(BF16)
    block_shapes = [((len(array) * slots.block, width), BF16) for array in slots.arrays]

    sent_grads = pl.pallas_call(
        functools.partial(dispatch_kernel, slots),
        in_specs=[SMEM] + [VMEM] * 3 + [ANY],
        out_specs=VMEM,
        out_shape=jax.ShapeDtypeStruct((n_expert * slots.block, width), BF16),
        compiler_params=params(),
        cost_estimate=SHORT,
    )(me_expert, places_row, others, cotangent, w_rel[0])
    got_grads = over_experts(sent_grads)
    far_tokens, _, w_pieces = lax.optimization_barrier((far_tokens, sent_grads, w_pieces))
    tree = [tokens, near_tokens, far_tokens, swap(far_tokens, "shard", 1)]

    place = lambda i, me_ref: (jnp.bitwise_xor(me_ref[0], i), 0)
    place_t = lambda i, me_ref: (0, jnp.bitwise_xor(me_ref[0], i))
    fixed = [
        ((width, wide), BF16), ((4, SEG, heads * SEG), F32), *[((1, width), F32)] * 2, ((width, n_experts), BF16),
    ]
    normed_one, queries, keys, values, keys_t, values_t, w_cols, bias, gain_one, gain_two, router_w = pl.pallas_call(
        functools.partial(project_kernel, heads),
        grid_spec=pltpu.PrefetchScalarGridSpec(
            num_scalar_prefetch=1,
            grid=(n_shard,),
            in_specs=[SMEM] + [VMEM] * 8 + [ANY],
            out_specs=[pl.BlockSpec((1, tok, width), lambda i, me_ref: (i, 0, 0))]
            + [pl.BlockSpec((tok, HW), place)] * 3
            + [pl.BlockSpec((HW, tok), place_t)] * 2
            + [pl.BlockSpec(shape, lambda i, me_ref, shape=shape: (0,) * len(shape)) for shape, _ in fixed],
            scratch_shapes=[pltpu.VMEM((width, 3 * HW + 128), BF16)],
        ),
        out_shape=arrays(
            ((n_shard, tok, width), BF16), *[((tree_len, HW), BF16)] * 3, *[((HW, tree_len), BF16)] * 2, *fixed
        ),
        compiler_params=params(dimension_semantics=("arbitrary",)),
        cost_estimate=SHORT,
    )(me_shard, rel_table.astype(F32), *w_pieces, *tree, sent_grads)
    parent_row = parents[0]
    *mixed, raw, lse = pl.pallas_call(
        functools.partial(attn_forward_kernel, heads),
        in_specs=[SMEM] * 2 + [VMEM] * 5,
        out_specs=[VMEM] * 6,
        out_shape=arrays(*[((hw, tok), BF16)] * 4, ((HW, tree_len), F32), ((SEGS * 8, heads * SEG), F32)),
        scratch_shapes=[pltpu.VMEM((HW, tree_len), BF16)],
        compiler_params=params(),
        cost_estimate=FORWARD,
    )(me_shard, parent_row, queries, keys, values, values_t, bias)
    first_far = swap(w_in[0], "shard", 2)
    w_o = lax.all_gather(w_output, "shard", axis=0)
    mixed, first_far, w_o = lax.optimization_barrier((mixed, first_far, w_o))
    mixed = swap_all(mixed, "shard")
    first_w = [w_in[0], swap(w_in[0], "shard", 1), first_far, swap(first_far, "shard", 1)]
    second_near = swap(w_out[0], "shard", 1)
    w_out, w_cols, _ = lax.optimization_barrier((w_out, w_cols, mixed))
    second_far = swap(w_out[0], "shard", 2)
    mixed, first_w, second_near = lax.optimization_barrier((mixed, first_w, second_near))

    after, normed_two, gates, *sent_rows = pl.pallas_call(
        functools.partial(post_kernel, slots),
        in_specs=[SMEM] + [VMEM] * 10,
        out_specs=[VMEM] * (3 + len(block_shapes)),
        out_shape=arrays(((tok, width), F32), ((tok, width), BF16), ((tok, 2), F32), *block_shapes),
        compiler_params=params(),
        cost_estimate=SHORT,
    )(me, tokens, gain_two, router_w, routes, places_row, *mixed, w_o)

    probs = pl.pallas_call(
        functools.partial(attn_prob_kernel, heads),
        in_specs=[SMEM] + [VMEM] * 4 + [ANY],
        out_specs=VMEM,
        out_shape=jax.ShapeDtypeStruct((PROB_ROWS, 2 * heads * SEG), BF16),
        compiler_params=params(),
        cost_estimate=SHORT,
    )(parent_row, queries, keys, lse, bias, after)

    second_far, probs = lax.optimization_barrier((second_far, probs))
    second_w = [w_out[0], second_near, second_far, swap(second_far, "shard", 1)]
    run = functools.partial(run_expert, slots)
    shared = (me, got_grads, router_w, first_w, second_w)
    near_rows = slots.near_exchange(sent_rows[0])
    if slots.cut:
        far_shape = sent_rows[1].shape
        out_all, own_dx, *own_kept = run("own", sent_rows[:1], far_shape, shared, [probs], SHORT)
        far_rows, probs = lax.optimization_barrier((sent_rows[1:], probs))
        far_rows = [swap(block, "expert", rel) for block, rel in zip(far_rows, slots.rels)]
        out_all, near_dx, *near_kept = run("near", [near_rows], near_rows.shape, shared, [probs, own_dx, out_all], SHORT)
        out_all, *far = run("far", far_rows, far_shape, shared, [probs, out_all], LONG)
        dx = [slots.near_exchange(near_dx)] + [swap(block, "expert", rel) for block, rel in zip(far, slots.rels)]
        kept = [own_kept, near_kept, far[4:]]
    else:
        out_all, dx, *all_kept = run("all", [near_rows], near_rows.shape, shared, [probs], SHORT)
        dx, kept = [slots.near_exchange(dx)], [all_kept]
    send_second, keep_second = run_second_grad([k[2] for k in kept], [k[1] for k in kept])
    w_cols, _ = lax.optimization_barrier((w_cols, kept[0][0]))
    w_all = lax.all_gather(w_cols, "shard", axis=0)
    send_first, keep_first = run_first_grad(me, [k[0] for k in kept], [k[3] for k in kept], rows, dx[0], w_all)
    out_all, _ = lax.optimization_barrier((out_all, dx[0]))
    returned = over_experts(out_all)
    dx, send_first, send_second = lax.optimization_barrier((dx, send_first, send_second))

    slot_rows = slots.n_expert * slots.block
    grad_after, gm0, gm1, gm2, gm3, send_wo, keep_wo = pl.pallas_call(
        functools.partial(back_kernel, slots),
        in_specs=[SMEM] + [VMEM] * (len(block_shapes) + 13),
        out_specs=[VMEM] * 7,
        out_shape=arrays(((tok, width), F32), *[((hw, tok), BF16)] * 4, *[((2 * rows, width + 128), BF16)] * 2),
        scratch_shapes=[
            pltpu.VMEM((tok, width), BF16),
            pltpu.VMEM((tok, n_experts), BF16),
            pltpu.VMEM((8, width), F32),
            pltpu.VMEM((width, 128), F32),
            pltpu.VMEM((slot_rows, width), BF16),
        ],
        compiler_params=params(),
        cost_estimate=SHORT,
    )(me_shard, *dx, places, routes, gates, after, gain_two, router_w, cotangent, w_o, normed_two, *mixed)
    grad_mixed = swap_all([gm0, gm1, gm2, gm3], "shard")
    sums = [
        core_sum(send, keep)
        for send, keep in ((send_second, keep_second), (send_first, keep_first), (send_wo, keep_wo))
    ]
    grad_mixed, sums = lax.optimization_barrier((grad_mixed, sums))
    second_sum, first_sum, wo_sum = sums
    second_sum, wo_sum = across_sum(second_sum), across_sum(wo_sum)

    *dqkv, bins = pl.pallas_call(
        functools.partial(attn_backward_kernel, heads),
        in_specs=[SMEM] * 2 + [VMEM] * 5 + [ANY] + [VMEM] * 4,
        out_specs=[VMEM] * 5,
        out_shape=arrays(*[((tok, wide), BF16)] * 4, ((NB, heads * SEG), F32)),
        scratch_shapes=[
            pltpu.VMEM((HW, tree_len), BF16),
            pltpu.VMEM((tree_len, HW), BF16),
            pltpu.VMEM((tree_len, HW), F32),
            pltpu.VMEM((tree_len, HW), F32),
            pltpu.VMEM((2, SEG, heads * SEG), F32),
            pltpu.VMEM((PROB_ROWS, 2 * heads * SEG), BF16),
            pltpu.SemaphoreType.DMA((SEGS // 2,)),
        ],
        compiler_params=params(),
        cost_estimate=BACKWARD,
    )(me_shard, parent_row, queries, keys, values, keys_t, raw, probs, *grad_mixed)
    dqkv_own = swap_all(dqkv, "shard")

    halving = [(1, 2, 4), (2, 1, 4)] if n_expert == 8 else []
    orders = [[0], [0]]
    for i, bits in enumerate(halving):
        for bit in reversed(bits):
            orders[i] = orders[i] + [rel | bit for rel in orders[i]]
    share = rows // len(orders[0])
    block_rows = [3 * share, 2 * share + -(-share // 16) * 8]
    parts = 2 if halving else 1
    out_rows = [count * len(orders[0]) // parts for count in block_rows for _ in range(parts)]
    halves = pl.pallas_call(
        functools.partial(column_grad_kernel, orders, heads),
        in_specs=[SMEM] + [VMEM] * 9,
        out_specs=[VMEM] * len(out_rows),
        out_shape=arrays(*[((count, wide), BF16) for count in out_rows]),
        scratch_shapes=[pltpu.VMEM((width, wide), F32), pltpu.VMEM((rows, width + 128), F32)],
        compiler_params=params(),
        cost_estimate=SHORT,
    )(me_expert if halving else jnp.zeros((1,), jnp.int32), bins, normed_one, *dqkv, *wo_sum)
    if halving:
        pairs = [halves[:2], halves[2:]]
        pairs, second_sum, returned = lax.optimization_barrier((pairs, second_sum, returned))
        for step in range(2):
            sums = [kept.astype(F32) + swap(sent, "expert", bits[step]).astype(F32) for (kept, sent), bits in zip(pairs, halving)]
            pairs = [jnp.split(part.astype(BF16), 2, axis=0) for part in sums]
        sums = [part for kept, sent in pairs for part in (kept, swap(sent, "expert", 4))]
    else:
        sums = lax.psum([part.astype(F32) for part in halves], "expert")
    *cols, more, table = pl.pallas_call(
        split_kernel,
        in_specs=[SMEM] + [VMEM] * len(sums),
        out_specs=[VMEM] * 6,
        out_shape=arrays(*[((share, 3 * hw), BF16)] * 4, ((share, width + 128), BF16), ((NB, wide - 3 * hw), F32)),
        scratch_shapes=[pltpu.VMEM((sum(block_rows), wide), F32)],
        compiler_params=params(),
        cost_estimate=SHORT,
    )(me_shard, *sums)
    table = table[:, :heads].T
    cols, dqkv_own = lax.optimization_barrier((cols, dqkv_own))
    cols, first_sum = lax.optimization_barrier((swap_all(cols, "shard"), first_sum))
    cols = pl.pallas_call(
        join_kernel,
        in_specs=[SMEM] + [VMEM] * 5,
        out_specs=VMEM,
        out_shape=jax.ShapeDtypeStruct((share, 4 * width + 128), BF16),
        compiler_params=params(),
        cost_estimate=SHORT,
    )(me_shard, *cols, more)
    grad_w_in = total_sum(across_sum(first_sum))[None]
    returned, second_sum, _ = lax.optimization_barrier((returned, second_sum, cols))
    grad_w_out = total_sum(second_sum)[None]
    output = pl.pallas_call(
        functools.partial(combine_kernel, slots),
        in_specs=[SMEM] + [VMEM] * 3,
        out_specs=VMEM,
        out_shape=jax.ShapeDtypeStruct((tok, width), BF16),
        scratch_shapes=[pltpu.VMEM((slot_rows, width), BF16)],
        compiler_params=params(),
        cost_estimate=SHORT,
    )(me_expert, returned, places, after)
    pieces = [cols]
    if halving:
        other = swap(cols, "expert", 4)
        dqkv_own, other = lax.optimization_barrier((dqkv_own, other))
        pieces = swap_all([jnp.concatenate([cols, other], axis=0)] * 4, "expert")
    grad_tokens = pl.pallas_call(
        final_kernel,
        in_specs=[SMEM] + [VMEM] * 8,
        out_specs=VMEM,
        out_shape=jax.ShapeDtypeStruct((tok, width), BF16),
        compiler_params=params(),
        cost_estimate=SHORT,
    )(me_shard, tokens, gain_one, grad_after, *dqkv_own, w_all)
    pieces, output, grad_tokens, grad_w_in, grad_w_out = lax.optimization_barrier(
        (pieces, output, grad_tokens, grad_w_in, grad_w_out)
    )
    grad_q, grad_k, grad_v, grad_wo, grad_router, grad_gains = pl.pallas_call(
        functools.partial(place_kernel, n_experts),
        in_specs=[SMEM] + [VMEM] * (4 + len(pieces)),
        out_specs=[VMEM] * 6,
        out_shape=arrays(*[((rows, width), F32)] * 4, ((n_experts, rows), F32), ((2, rows), F32)),
        scratch_shapes=[pltpu.VMEM((rows, 128), F32)],
        compiler_params=params(),
        cost_estimate=SHORT,
    )(
        me_expert if halving else jnp.zeros((1,), jnp.int32), w_query, w_key, w_value,
        gain_attn.astype(F32).reshape(1, rows), *pieces,
    )

    return (
        output, grad_tokens, grad_gains[0], grad_q, grad_k, grad_v, grad_wo, table, grad_gains[1], grad_router.T,
        grad_w_in, grad_w_out,
    )


def solution(mesh):
    both, shard = P(("expert", "shard"), None), P("shard", None)
    three = P("expert", "shard", None)
    return jax.shard_map(
        per_device,
        mesh=mesh,
        in_specs=(
            both, P("shard"), shard, shard, shard, shard, shard, P("shard"), shard, three, three, both,
            P("expert", None), both,
        ),
        out_specs=(both, both, P("shard"), shard, shard, shard, shard, shard, P("shard"), shard, three, three),
        check_vma=False,
    )
```

profile of v0, /device:TPU:0, one launch (start us, length us, event | category | flops | bytes accessed | tf_op | source)
XLA Modules:
  0.0 411.1 jit_solution(16922482573210025477)
XLA Ops:
  23.6 8.2 %shard_map.230.before_ref = bf16[1920,768]{1,0:T(8,128)(2,1)} custom-call(s32[1]{0:T(128)} %bitcast.1.me_ref, s32[2,640]{1,0:T(2,128)} %copy.72.places_ref, bf16[16,640]{1,0:T(8,128)(2,1)} %broadcast_bitcast_fusion.others_ref, bf16[640,768]{1,0:T(8,128)(2,1)} %refs_11_.1, bf16[192,640]{1,0:T(8,128)(2,1)} %get-tuple-element.189.refs_0_.w0), custom_call_target="tpu_custom_call" | custom-call | bytes 1024 | tf_op jit(solution)/shard_map/pallas_call | solution.py:1012
  31.7 5.8 %all-to-all-start.1 = ((bf16[8,240,768]{2,1,0:T(8,128)(2,1)}), bf16[8,240,768]{2,1,0:T(8,128)(2,1)S(1)}, u32[]{:S(2)}, u32[]{:S(2)}) async-start(bf16[8,240,768]{2,1,0:T(8,128)(2,1)} %bitcast.52), calls=%async_computation.1 | async-start | bytes 5898240 | tf_op jit(solution)/shard_map/all_to_all | solution.py:433
  45.8 10.6 %shard_map.231 = (bf16[4,640,768]{2,1,0:T(8,128)(2,1)}, bf16[2560,256]{1,0:T(8,128)(2,1)}, bf16[2560,256]{1,0:T(8,128)(2,1)}, bf16[2560,256]{1,0:T(8,128)(2,1)},...) custom-call(s32[1]{0:T(128)} %bitcast.me_ref, ...), custom_call_target="tpu_custom_call" | custom-call | bytes 1024 | tf_op jit(solution)/shard_map/pallas_call | solution.py:1029
  56.3 20.4 %shard_map.232 = (bf16[192,640]{1,0:T(8,128)(2,1)}, bf16[192,640]{1,0:T(8,128)(2,1)}, bf16[192,640]{1,0:T(8,128)(2,1)}, bf16[192,640]{1,0:T(8,128)(2,1)}, f32[256,2560]{1,0:T(8,128)}, /*index=5*/f32[160,384]{1,0:T(8,128)}) custom-call(s32[1]{0:T(128)} %bitcast.me_ref, s32[20]{0:T(128)} %bitcast.77, bf16[2560,256]{1,0:T(8,128)(2,1)} %get-tuple-element.194.q_ref, ...), custom_call_target="tpu_custom_call" | custom-call | flops 30400000000 | bytes 1024 | tf_op jit(solution)/shard_map/pallas_call | solution.py:1048
  82.1 4.8 %collective-permute-done.8.m2.refs_16_ = bf16[192,640]{1,0:T(8,128)(2,1)S(1)} collective-permute-done((bf16[192,640]{1,0:T(8,128)(2,1)}, bf16[192,640]{1,0:T(8,128)(2,1)S(1)}, u32[]{:S(2)}, u32[]{:S(2)}) %collective-permute-start.8) | collective-permute-done | bytes 245792 | tf_op jit(solution)/shard_map/ppermute | solution.py:439
  92.7 7.2 %shard_map.233 = (f32[640,768]{1,0:T(8,128)}, bf16[640,768]{1,0:T(8,128)(2,1)}, f32[640,2]{1,0:T(8,128)}, bf16[960,768]{1,0:T(8,128)(2,1)}, bf16[240,768]{1,0:T(...) custom-call(s32[2]{0:T(128)} %pad_add_fusion.me_ref, ...), custom_call_target="tpu_custom_call" | custom-call | bytes 1024 | tf_op jit(solution)/shard_map/pallas_call | solution.py:1067
  99.9 4.6 %all-to-all-done.1 = bf16[8,240,768]{2,1,0:T(8,128)(2,1)S(1)} async-done(((bf16[8,240,768]{2,1,0:T(8,128)(2,1)}), bf16[8,240,768]{2,1,0:T(8,128)(2,1)S(1)}, u32[]{:S(2)}, u32[]{:S(2)}) %all-to-all-start.1) | async-done | bytes 2949152 | tf_op jit(solution)/shard_map/all_to_all | solution.py:433
  104.5 4.3 %all-to-all-start = ((bf16[4,240,768]{2,1,0:T(8,128)(2,1)}), bf16[4,240,768]{2,1,0:T(8,128)(2,1)}, u32[]{:S(2)}, u32[]{:S(2)}) async-start(bf16[4,240,768]{2,1,0:T(8,128)(2,1)} %bitcast.57), calls=%async_computation | async-start | bytes 2949120 | tf_op jit(solution)/shard_map/all_to_all | solution.py:429
  108.9 14.3 %shard_map.234.refs_11_.refs_14_.prob_ref = bf16[10240,768]{1,0:T(8,128)(2,1)} custom-call(s32[20]{0:T(128)} %bitcast.78, bf16[2560,256]{1,0:T(8,128)(2,1)} %get-tuple-element.194.q_ref, bf16[2560,256]{1,0:T(8,128)(2,1)} %get-tuple-element.195.k_ref, f32[160,384]{1,0:T(8,128)} %get-tuple-element.223.lse_ref, f32[4,128,384]{2,1,0:T(8,128)} %get-tuple-element.199.bias_ref, ...), custom_call_target="tpu_custom_call" | custom-call | bytes 1024 | tf_op jit(solution)/shard_map/pallas_call | solution.py:1076
  131.2 12.9 %shard_map.235 = (bf16[1920,768]{1,0:T(8,128)(2,1)}, bf16[240,768]{1,0:T(8,128)(2,1)}, bf16[240,768]{1,0:T(8,128)(2,1)}, bf16[240,768]{1,0:T(8,128)(2,1)}, bf16[...) custom-call(s32[2]{0:T(128)} %pad_add_fusion.me_ref, bf16[960,768]{1,0:T(8,128)(2,1)} %get-tuple-element.227.refs_0_, ...), custom_call_target="tpu_custom_call" | custom-call | bytes 1024 | tf_op jit(solution)/shard_map/pallas_call | solution.py:680
  144.1 26.3 %shard_map.236 = (bf16[1920,768]{1,0:T(8,128)(2,1)}, bf16[960,768]{1,0:T(8,128)(2,1)}, bf16[720,768]{1,0:T(8,128)(2,1)}, bf16[720,768]{1,0:T(8,128)(2,1)}, bf16[...) custom-call(s32[2]{0:T(128)} %pad_add_fusion.me_ref, ...), custom_call_target="tpu_custom_call", output_to_operand_aliasing={{0}: (14, {})} | custom-call | bytes 1024 | tf_op jit(solution)/shard_map/pallas_call | solution.py:680
  170.4 4.5 %all-to-all-start.2 = ((bf16[4,240,768]{2,1,0:T(8,128)(2,1)}), bf16[4,240,768]{2,1,0:T(8,128)(2,1)}, u32[]{:S(2)}, u32[]{:S(2)}) async-start(bf16[4,240,768]{2,1,0:T(8,128)(2,1)} %bitcast.71), calls=%async_computation.2 | async-start | bytes 2949120 | tf_op jit(solution)/shard_map/all_to_all | solution.py:429
  176.2 31.1 %shard_map.237 = (bf16[1920,768]{1,0:T(8,128)(2,1)}, bf16[240,768]{1,0:T(8,128)(2,1)}, bf16[240,768]{1,0:T(8,128)(2,1)}, bf16[240,768]{1,0:T(8,128)(2,1)}, bf16[...) custom-call(s32[2]{0:T(128)} %pad_add_fusion.me_ref, ...), custom_call_target="tpu_custom_call", output_to_operand_aliasing={{0}: (16, {})} | custom-call | flops 1099511627776 | bytes 4294967296 | tf_op jit(solution)/shard_map/pallas_call | solution.py:680
  214.2 15.7 %shard_map.239 = (bf16[1536,768]{1,0:T(8,128)(2,1)}, bf16[1536,768]{1,0:T(8,128)(2,1)}) custom-call(bf16[240,3072]{1,0:T(8,128)(2,1)} %get-tuple-element.255.refs_0_, bf16[720,3072]{1,0:T(8,128)(2,1)} %get-tuple-element.256.refs_1_, bf16[960,3072]{1,0:T(8,128)(2,1)} %get-tuple-element.257.refs_2_, bf16[240,768]{1,0:T(8,128)(2,1)} %get-tuple-element.258.refs_3_, ...), custom_call_target="tpu_custom_call" | custom-call | bytes 1024 | tf_op jit(solution)/shard_map/pallas_call | solution.py:755
  229.9 15.9 %shard_map.238 = (bf16[384,3072]{1,0:T(8,128)(2,1)}, bf16[384,3072]{1,0:T(8,128)(2,1)}) custom-call(s32[2]{0:T(128)} %pad_add_fusion.me_ref, bf16[240,768]{1,0:T(8,128)(2,1)} %get-tuple-element.246.refs_0_, bf16[720,768]{1,0:T(8,128)(2,1)} %get-tuple-element.247.refs_1_, bf16[960,768]{1,0:T(8,128)(2,1)} %get-tuple-element.248.refs_2_, ...), custom_call_target="tpu_custom_call" | custom-call | bytes 1024 | tf_op jit(solution)/shard_map/pallas_call | solution.py:721
  247.1 5.1 %all-to-all-start.3 = ((bf16[8,240,768]{2,1,0:T(8,128)(2,1)}), bf16[8,240,768]{2,1,0:T(8,128)(2,1)S(1)}, u32[]{:S(2)}, u32[]{:S(2)}) async-start(bf16[8,240,768]{2,1,0:T(8,128)(2,1)} %bitcast.56), calls=%async_computation.3 | async-start | bytes 5898240 | tf_op jit(solution)/shard_map/all_to_all | solution.py:433
  252.3 13.0 %shard_map.240 = (f32[640,768]{1,0:T(8,128)}, bf16[192,640]{1,0:T(8,128)(2,1)}, bf16[192,640]{1,0:T(8,128)(2,1)}, bf16[192,640]{1,0:T(8,128)(2,1)}, bf16[192,640...) custom-call(s32[1]{0:T(128)} %bitcast.me_ref, bf16[960,768]{1,0:T(8,128)(2,1)} %bitcast.16.refs_6_.refs_0_, ...), custom_call_target="tpu_custom_call" | custom-call | bytes 1024 | tf_op jit(solution)/shard_map/pallas_call | solution.py:1111
  281.3 28.7 %shard_map.241 = (bf16[640,640]{1,0:T(8,128)(2,1)}, bf16[640,640]{1,0:T(8,128)(2,1)}, bf16[640,640]{1,0:T(8,128)(2,1)}, bf16[640,640]{1,0:T(8,128)(2,1)}, f32[16,384]{1,0:T(8,128)}) custom-call(s32[1]{0:T(128)} %bitcast.me_ref, s32[20]{0:T(128)} %bitcast.79, bf16[2560,256]{1,0:T(8,128)(2,1)} %get-tuple-element.194.q_ref, ...), custom_call_target="tpu_custom_call" | custom-call | flops 22000001024 | bytes 1024 | tf_op jit(solution)/shard_map/pallas_call | solution.py:1135
  310.8 8.4 %shard_map.242 = (bf16[288,640]{1,0:T(8,128)(2,1)}, bf16[288,640]{1,0:T(8,128)(2,1)}, bf16[256,640]{1,0:T(8,128)(2,1)}, bf16[256,640]{1,0:T(8,128)(2,1)}) custom-call(s32[1]{0:T(128)} %bitcast.1.me_ref, f32[16,384]{1,0:T(8,128)} %get-tuple-element.283.bins_ref, bf16[4,640,768]{2,1,0:T(8,128)(2,1)} %get-tuple-element.284.n_ref, ...), custom_call_target="tpu_custom_call" | custom-call | bytes 1024 | tf_op jit(solution)/shard_map/pallas_call | solution.py:1163
  324.5 4.8 %collective-permute-done.34 = bf16[256,640]{1,0:T(8,128)(2,1)S(1)} collective-permute-done((bf16[256,640]{1,0:T(8,128)(2,1)}, bf16[256,640]{1,0:T(8,128)(2,1)S(1)}, u32[]{:S(2)}, u32[]{:S(2)}) %collective-permute-start.34) | collective-permute-done | bytes 327712 | tf_op jit(solution)/shard_map/ppermute | solution.py:439
  343.2 6.4 %collective-permute-done.36.refs_3_ = bf16[64,640]{1,0:T(8,128)(2,1)S(1)} collective-permute-done((bf16[64,640]{1,0:T(8,128)(2,1)S(1)}, bf16[64,640]{1,0:T(8,128)(2,1)S(1)}, u32[]{:S(2)}, u32[]{:S(2)}) %collective-permute-start.36) | collective-permute-done | bytes 81952 | tf_op jit(solution)/shard_map/ppermute | solution.py:439
  352.0 8.8 %collective-permute-done.39.d3 = bf16[640,640]{1,0:T(8,128)(2,1)} collective-permute-done((bf16[640,640]{1,0:T(8,128)(2,1)}, bf16[640,640]{1,0:T(8,128)(2,1)}, u32[]{:S(2)}, u32[]{:S(2)}) %collective-permute-start.39) | collective-permute-done | bytes 819232 | tf_op jit(solution)/shard_map/ppermute | solution.py:439
  376.4 6.6 %shard_map.245 = bf16[640,768]{1,0:T(8,128)(2,1)} custom-call(s32[1]{0:T(128)} %bitcast.1.me_ref, bf16[1920,768]{1,0:T(8,128)(2,1)} %bitcast.55, s32[640,2]{1,0:T(8,128)} %copy-done.3, f32[640,768]{1,0:T(8,128)} %get-tuple-element.224.before_ref.refs_8_.after_ref), custom_call_target="tpu_custom_call" | custom-call | bytes 1024 | tf_op jit(solution)/shard_map/pallas_call | solution.py:1204
  386.6 8.8 %shard_map.246 = bf16[640,768]{1,0:T(8,128)(2,1)} custom-call(s32[1]{0:T(128)} %bitcast.me_ref, bf16[640,768]{1,0:T(8,128)(2,1)} %x_ref.3, f32[1,768]{1,0:T(1,128)} %get-tuple-element.331.gain_ref, f32[640,768]{1,0:T(8,128)} %get-tuple-element.332.after_ref, bf16[640,640]{1,0:T(8,128)(2,1)} %get-tuple-element.333.d0, ...), custom_call_target="tpu_custom_call" | custom-call | bytes 1024 | tf_op jit(solution)/shard_map/pallas_call | solution.py:1218
  (216 shorter events, 119.2 us)
Async XLA Ops:
  7.2 34.9 %collective-permute-start = (bf16[640,768]{1,0:T(8,128)(2,1)}, bf16[640,768]{1,0:T(8,128)(2,1)}, u32[]{:S(2)}, u32[]{:S(2)}) collective-permute-start(bf16[640,768]{1,0:T(8,128)(2,1)} %x_ref.3), channel_id=1, source_target_pairs={{0,2},{1,3},{2,0},{3,1},{4,6},{5,7},{6,4},{7,5},{8,10},{9,11},{10,... | collective-permute-start | bytes 2949128 | tf_op jit(solution)/shard_map/ppermute | solution.py:439
  31.7 72.8 %all-to-all-start.1 = ((bf16[8,240,768]{2,1,0:T(8,128)(2,1)}), bf16[8,240,768]{2,1,0:T(8,128)(2,1)S(1)}, u32[]{:S(2)}, u32[]{:S(2)}) async-start(bf16[8,240,768]{2,1,0:T(8,128)(2,1)} %bitcast.52), calls=%async_computation.1 | async-start | bytes 5898240 | tf_op jit(solution)/shard_map/all_to_all | solution.py:433
  37.6 39.7 %all-gather.5.cloned.1.call-start = ((), (), s32[]{:S(2)}) async-start(), calls=%async_computation.4 | async-start | bytes 1474560 | tf_op jit(solution)/shard_map/all_gather | solution.py:1058
  42.8 34.5 %collective-permute-start.6 = (bf16[192,3072]{1,0:T(8,128)(2,1)}, bf16[192,3072]{1,0:T(8,128)(2,1)}, u32[]{:S(2)}, u32[]{:S(2)}) collective-permute-start(bf16[192,3072]{1,0:T(8,128)(2,1)} %bitcast.59), channel_id=1, source_target_pairs={{0,2},{1,3},{2,0},{3,1},{4,6},{5,7},{6,4},{7,5},{8,10},{9,11},{10,... | collective-permute-start | bytes 3538952 | tf_op jit(solution)/shard_map/ppermute | solution.py:439
  44.6 48.1 %collective-permute-start.10 = (bf16[192,3072]{1,0:T(8,128)(2,1)}, bf16[192,3072]{1,0:T(8,128)(2,1)}, u32[]{:S(2)}, u32[]{:S(2)}) collective-permute-start(bf16[192,3072]{1,0:T(8,128)(2,1)} %bitcast.60), channel_id=1, source_target_pairs={{0,1},{1,0},{2,3},{3,2},{4,5},{5,4},{6,7},{7,6},{8,9},{9,8},{10,11... | collective-permute-start | bytes 3538952 | tf_op jit(solution)/shard_map/ppermute | solution.py:439
  44.6 48.1 %collective-permute-start.12 = (bf16[768,768]{1,0:T(8,128)(2,1)}, bf16[768,768]{1,0:T(8,128)(2,1)}, u32[]{:S(2)}, u32[]{:S(2)}) collective-permute-start(bf16[768,768]{1,0:T(8,128)(2,1)} %bitcast.64), channel_id=1, source_target_pairs={{0,1},{1,0},{2,3},{3,2},{4,5},{5,4},{6,7},{7,6},{8,9},{9,8},{10,11... | collective-permute-start | bytes 3538952 | tf_op jit(solution)/shard_map/ppermute | solution.py:439
  90.5 32.6 %collective-permute-start.13 = (bf16[768,768]{1,0:T(8,128)(2,1)}, bf16[768,768]{1,0:T(8,128)(2,1)}, u32[]{:S(2)}, u32[]{:S(2)}) collective-permute-start(bf16[768,768]{1,0:T(8,128)(2,1)} %bitcast.65), channel_id=1, source_target_pairs={{0,2},{1,3},{2,0},{3,1},{4,6},{5,7},{6,4},{7,5},{8,10},{9,11},{10,... | collective-permute-start | bytes 3538952 | tf_op jit(solution)/shard_map/ppermute | solution.py:439
  104.5 39.6 %all-to-all-start = ((bf16[4,240,768]{2,1,0:T(8,128)(2,1)}), bf16[4,240,768]{2,1,0:T(8,128)(2,1)}, u32[]{:S(2)}, u32[]{:S(2)}) async-start(bf16[4,240,768]{2,1,0:T(8,128)(2,1)} %bitcast.57), calls=%async_computation | async-start | bytes 2949120 | tf_op jit(solution)/shard_map/all_to_all | solution.py:429
  108.9 121.1 %all-gather.7.cloned.1.call-start = ((), (), s32[]{:S(2)}) async-start(), calls=%async_computation.5 | async-start | bytes 4915200 | tf_op jit(solution)/shard_map/all_gather | solution.py:1104
  123.3 51.7 %collective-permute-start.15 = (bf16[240,768]{1,0:T(8,128)(2,1)}, bf16[240,768]{1,0:T(8,128)(2,1)S(1)}, u32[]{:S(2)}, u32[]{:S(2)}) collective-permute-start(bf16[240,768]{1,0:T(8,128)(2,1)} %get-tuple-element.237), channel_id=1, source_target_pairs={{0,8},{4,12},{8,0},{12,4},{16,24},{20,28},{24,16},{28,20},{1,9},{5... | collective-permute-start | bytes 1105928 | tf_op jit(solution)/shard_map/ppermute | solution.py:439
  123.3 51.9 %collective-permute-start.16 = (bf16[240,768]{1,0:T(8,128)(2,1)}, bf16[240,768]{1,0:T(8,128)(2,1)S(1)}, u32[]{:S(2)}, u32[]{:S(2)}) collective-permute-start(bf16[240,768]{1,0:T(8,128)(2,1)} %get-tuple-element.238), channel_id=1, source_target_pairs={{0,12},{4,8},{8,4},{12,0},{16,28},{20,24},{24,20},{28,16},{1,13},{... | collective-permute-start | bytes 1105928 | tf_op jit(solution)/shard_map/ppermute | solution.py:439
  126.7 48.5 %collective-permute-start.17 = (bf16[240,768]{1,0:T(8,128)(2,1)}, bf16[240,768]{1,0:T(8,128)(2,1)S(1)}, u32[]{:S(2)}, u32[]{:S(2)}) collective-permute-start(bf16[240,768]{1,0:T(8,128)(2,1)} %get-tuple-element.239), channel_id=1, source_target_pairs={{0,24},{4,28},{8,16},{12,20},{16,8},{20,12},{24,0},{28,4},{1,25},{... | collective-permute-start | bytes 1105928 | tf_op jit(solution)/shard_map/ppermute | solution.py:439
  128.6 46.6 %collective-permute-start.18 = (bf16[240,768]{1,0:T(8,128)(2,1)S(1)}, bf16[240,768]{1,0:T(8,128)(2,1)S(1)}, u32[]{:S(2)}, u32[]{:S(2)}) collective-permute-start(bf16[240,768]{1,0:T(8,128)(2,1)S(1)} %copy-done.26), channel_id=1, source_target_pairs={{0,28},{4,24},{8,20},{12,16},{16,12},{20,8},{24,4},{28,0},{1,29},{... | collective-permute-start | bytes 1105928 | tf_op jit(solution)/shard_map/ppermute | solution.py:439
  170.4 59.5 %all-to-all-start.2 = ((bf16[4,240,768]{2,1,0:T(8,128)(2,1)}), bf16[4,240,768]{2,1,0:T(8,128)(2,1)}, u32[]{:S(2)}, u32[]{:S(2)}) async-start(bf16[4,240,768]{2,1,0:T(8,128)(2,1)} %bitcast.71), calls=%async_computation.2 | async-start | bytes 2949120 | tf_op jit(solution)/shard_map/all_to_all | solution.py:429
  207.4 38.5 %collective-permute-start.19 = (bf16[240,768]{1,0:T(8,128)(2,1)}, bf16[240,768]{1,0:T(8,128)(2,1)S(1)}, u32[]{:S(2)}, u32[]{:S(2)}) collective-permute-start(bf16[240,768]{1,0:T(8,128)(2,1)} %get-tuple-element.242), channel_id=1, source_target_pairs={{0,8},{4,12},{8,0},{12,4},{16,24},{20,28},{24,16},{28,20},{1,9},{5... | collective-permute-start | bytes 1105928 | tf_op jit(solution)/shard_map/ppermute | solution.py:439
  208.2 37.6 %collective-permute-start.20 = (bf16[240,768]{1,0:T(8,128)(2,1)}, bf16[240,768]{1,0:T(8,128)(2,1)S(1)}, u32[]{:S(2)}, u32[]{:S(2)}) collective-permute-start(bf16[240,768]{1,0:T(8,128)(2,1)} %get-tuple-element.243), channel_id=1, source_target_pairs={{0,12},{4,8},{8,4},{12,0},{16,28},{20,24},{24,20},{28,16},{1,13},{... | collective-permute-start | bytes 1105928 | tf_op jit(solution)/shard_map/ppermute | solution.py:439
  210.7 35.2 %collective-permute-start.21 = (bf16[240,768]{1,0:T(8,128)(2,1)}, bf16[240,768]{1,0:T(8,128)(2,1)S(1)}, u32[]{:S(2)}, u32[]{:S(2)}) collective-permute-start(bf16[240,768]{1,0:T(8,128)(2,1)} %get-tuple-element.244), channel_id=1, source_target_pairs={{0,24},{4,28},{8,16},{12,20},{16,8},{20,12},{24,0},{28,4},{1,25},{... | collective-permute-start | bytes 1105928 | tf_op jit(solution)/shard_map/ppermute | solution.py:439
  213.2 33.2 %collective-permute-start.22 = (bf16[240,768]{1,0:T(8,128)(2,1)}, bf16[240,768]{1,0:T(8,128)(2,1)S(1)}, u32[]{:S(2)}, u32[]{:S(2)}) collective-permute-start(bf16[240,768]{1,0:T(8,128)(2,1)} %get-tuple-element.245), channel_id=1, source_target_pairs={{0,28},{4,24},{8,20},{12,16},{16,12},{20,8},{24,4},{28,0},{1,29},{... | collective-permute-start | bytes 1105928 | tf_op jit(solution)/shard_map/ppermute | solution.py:439
  247.1 72.0 %all-to-all-start.3 = ((bf16[8,240,768]{2,1,0:T(8,128)(2,1)}), bf16[8,240,768]{2,1,0:T(8,128)(2,1)S(1)}, u32[]{:S(2)}, u32[]{:S(2)}) async-start(bf16[8,240,768]{2,1,0:T(8,128)(2,1)} %bitcast.56), calls=%async_computation.3 | async-start | bytes 5898240 | tf_op jit(solution)/shard_map/all_to_all | solution.py:433
  279.3 30.7 %collective-permute-start.29 = (bf16[192,896]{1,0:T(8,128)(2,1)S(1)}, bf16[192,896]{1,0:T(8,128)(2,1)S(1)}, u32[]{:S(2)}, u32[]{:S(2)}) collective-permute-start(bf16[192,896]{1,0:T(8,128)(2,1)S(1)} %add_convert_fusion.3), channel_id=1, source_target_pairs={{0,2},{1,3},{2,0},{3,1},{4,6},{5,7},{6,4},{7,5},{8,10},{9,11},{10,... | collective-permute-start | bytes 1032200 | tf_op jit(solution)/shard_map/ppermute | solution.py:439
  280.0 39.1 %collective-permute-start.30 = (bf16[768,768]{1,0:T(8,128)(2,1)}, bf16[768,768]{1,0:T(8,128)(2,1)}, u32[]{:S(2)}, u32[]{:S(2)}) collective-permute-start(bf16[768,768]{1,0:T(8,128)(2,1)} %add_convert_fusion.1), channel_id=1, source_target_pairs={{0,2},{1,3},{2,0},{3,1},{4,6},{5,7},{6,4},{7,5},{8,10},{9,11},{10,... | collective-permute-start | bytes 3538952 | tf_op jit(solution)/shard_map/ppermute | solution.py:439
  322.7 29.3 %collective-permute-start.38 = (bf16[640,640]{1,0:T(8,128)(2,1)}, bf16[640,640]{1,0:T(8,128)(2,1)}, u32[]{:S(2)}, u32[]{:S(2)}) collective-permute-start(bf16[640,640]{1,0:T(8,128)(2,1)} %get-tuple-element.287.d2), channel_id=1, source_target_pairs={{0,2},{1,3},{2,0},{3,1},{4,6},{5,7},{6,4},{7,5},{8,10},{9,11},{10,... | collective-permute-start | bytes 2457608 | tf_op jit(solution)/shard_map/ppermute | solution.py:439
  323.4 37.4 %collective-permute-start.39 = (bf16[640,640]{1,0:T(8,128)(2,1)}, bf16[640,640]{1,0:T(8,128)(2,1)}, u32[]{:S(2)}, u32[]{:S(2)}) collective-permute-start(bf16[640,640]{1,0:T(8,128)(2,1)} %get-tuple-element.288.d3), channel_id=1, source_target_pairs={{0,3},{1,2},{2,1},{3,0},{4,7},{5,6},{6,5},{7,4},{8,11},{9,10},{10,... | collective-permute-start | bytes 2457608 | tf_op jit(solution)/shard_map/ppermute | solution.py:439
  365.6 29.8 %collective-permute-start.47 = (bf16[192,3072]{1,0:T(8,128)(2,1)}, bf16[192,3072]{1,0:T(8,128)(2,1)S(1)}, u32[]{:S(2)}, u32[]{:S(2)}) collective-permute-start(bf16[192,3072]{1,0:T(8,128)(2,1)} %add_convert_fusion), channel_id=1, source_target_pairs={{0,2},{1,3},{2,0},{3,1},{4,6},{5,7},{6,4},{7,5},{8,10},{9,11},{10,... | collective-permute-start | bytes 3538952 | tf_op jit(solution)/shard_map/ppermute | solution.py:439
  (65 other events, 625.2 us)
Sparse Core Ops, SparseCore 0:
  44.7 24.3 all-gather.4
  144.2 31.9 all-gather.6
where the time goes:
time: 415 us; the launch traced here: 411 us
  Pallas kernels  237 us (57%)
  starting transfers between devices  71.9 us (17%)
  waiting for transfers between devices  52.3 us (13%)
  other arithmetic  21.1 us (5%)
  between operations  14.8 us (4%)
  local copies, waits for them, and re-layouts  14.1 us (3%)
    pallas_call x3, Pallas kernels, run_expert(): pl.pallas_call(functools.partial(expert_kernel, slots, kind, (len(blocks)...  70.3 us
    ppermute x48, starting transfers between devices, swap(): lax.ppermute(block, axis, [(i, i ^ rel) for i in range(lax.axis_size(axis...  51.8 us
    ppermute x48, waiting for transfers between devices, swap(): lax.ppermute(block, axis, [(i, i ^ rel) for i in range(lax.axis_size(axis...  47.7 us
    pallas_call x1, Pallas kernels, per_device(): pl.pallas_call(functools.partial(attn_backward_kernel, heads), in_specs=[...  28.7 us
    pallas_call x1, Pallas kernels, per_device(): pl.pallas_call(functools.partial(attn_forward_kernel, heads), in_specs=[S...  20.4 us
    pallas_call x1, Pallas kernels, run_first_grad(): pl.pallas_call(functools.partial(first_grad_kernel, len(rows)), grid_spec...  15.9 us
    pallas_call x1, Pallas kernels, run_second_grad(): pl.pallas_call(functools.partial(second_grad_kernel, len(acts)), grid=(4,...  15.7 us
    pallas_call x1, Pallas kernels, per_device(): pl.pallas_call(functools.partial(attn_prob_kernel, heads), in_specs=[SMEM...  14.3 us
  transfers between devices with their start and end apart: 54, of which 19 were waited for; matrix products, arithmetic and copies ran while one was open for 7% of the time, Pallas kernels for 57%

commit v1 on v0

--- a/solution.py
+++ b/solution.py
@@ -530,7 +530,7 @@
     own_ref = extra[1] if before == 3 else None
     (out_all,) = take(1)
     dx_refs = take(sizes[1])
-    rows_ref, grad_ref, act_ref, inner_ref, first_buf, second_buf, g_buf, out_buf, out_acc, dx_acc, gate_acc, gates_acc, sem, in_sem = refs
+    rows_out, grad_out, act_ref, inner_ref, rows_ref, grad_ref, first_buf, second_buf, g_buf, out_buf, out_acc, dx_acc, gate_acc, gates_acc, sem, in_sem, keep_sem = refs
     step = pl.program_id(0)
     slot = lax.rem(step, 2)
     total, width = rows_ref.shape
@@ -604,6 +604,16 @@
             gate_acc[at, :] = jnp.broadcast_to(gate, (rows, 128))
             grad_ref[at, :] = jnp.where(line < rows - SPARE, gate * grads, 0.0).astype(BF16)
 
+    keeps = [
+        pltpu.make_async_copy(rows_ref, rows_out, keep_sem.at[0]),
+        pltpu.make_async_copy(grad_ref, grad_out, keep_sem.at[1]),
+    ]
+
+    @pl.when(step == 0)
+    def _():
+        for copy in keeps:
+            copy.start()
+
     for rel in range(4):
         @pl.when(step == rel)
         def _(rel=rel):
@@ -659,7 +669,7 @@
                 gates = gates - piece
                 tail = jnp.where(line == 16 - SPARE + place, padded_row(piece, width), tail)
             dx_ref[row_at(inside + rows - 16, 16), :] = tail.astype(BF16)
-        for copy in copies:
+        for copy in [*copies, *keeps]:
             copy.wait()
 
 
@@ -670,7 +680,6 @@
     block = hidden // 4
     whole = lambda a: pl.BlockSpec(a.shape, lambda i: (0, 0))
     column = pl.BlockSpec((total, block), lambda i: (0, i))
-    rows = pl.BlockSpec((total, width), lambda i: (0, 0))
     fresh = len(before) < 2
     dx = [jax.ShapeDtypeStruct(dx_shape, BF16)] * (4 if kind == "far" else 1)
     inputs = [me, *blocks, g_all, router, *first_w, *second_w, *before]
@@ -681,11 +690,13 @@
         functools.partial(expert_kernel, slots, kind, (len(blocks), len(dx)), len(before)),
         grid=(4,),
         in_specs=[SMEM] + [whole(b) for b in blocks] + [ANY, whole(router)] + [ANY] * 8 + before_specs,
-        out_specs=[ANY] + [whole(b) for b in dx] + [rows, rows, column, column],
+        out_specs=[ANY] + [whole(b) for b in dx] + [ANY, ANY, column, column],
         out_shape=arrays(
             (g_all.shape, BF16), *[(b.shape, BF16) for b in dx], *[((total, width), BF16)] * 2, *[((total, hidden), BF16)] * 2
         ),
         scratch_shapes=[
+            pltpu.VMEM((total, width), BF16),
+            pltpu.VMEM((total, width), BF16),
             pltpu.VMEM((2, width, block), BF16),
             pltpu.VMEM((2, block, width), BF16),
             pltpu.VMEM((total, width), BF16),
@@ -696,6 +707,7 @@
             pltpu.VMEM((total, 128), F32),
             pltpu.SemaphoreType.DMA((total // slots.block,)),
             pltpu.SemaphoreType.DMA((2, 5)),
+            pltpu.SemaphoreType.DMA((2,)),
         ],
         input_output_aliases={} if fresh else {len(inputs) - 1: 0},
         compiler_params=params(dimension_semantics=("arbitrary",)),
@@ -1188,8 +1200,8 @@
         cost_estimate=SHORT,
     )(me_shard, *sums)
     table = table[:, :heads].T
-    cols, dqkv_own = lax.optimization_barrier((cols, dqkv_own))
-    cols, first_sum = lax.optimization_barrier((swap_all(cols, "shard"), first_sum))
+    cols, dqkv_own[2] = lax.optimization_barrier((cols, dqkv_own[2]))
+    cols, first_sum, dqkv_own = lax.optimization_barrier((swap_all(cols, "shard"), first_sum, dqkv_own))
     cols = pl.pallas_call(
         join_kernel,
         in_specs=[SMEM] + [VMEM] * 5,

time: 415 us -> 409 us (0.986)
  waiting for transfers between devices: 52.3 us -> 48.1 us
    ppermute x48, waiting for transfers between devices: 47.7 us -> 43.2 us  [swap(): lax.ppermute(block, axis, [(i, i ^ rel) for i in range(lax.axis_size(axis...]
  transfers between devices with their start and end apart: 54 -> 54, of which waited for: 19 -> 18; matrix products, arithmetic and copies ran while one was open for 7% -> 7% of each run, Pallas kernels for 57% -> 57%
where the time goes in v1:
time: 409 us; the launch traced here: 405 us
  Pallas kernels  235 us (57%)
  starting transfers between devices  71.6 us (18%)
  waiting for transfers between devices  48.1 us (12%)
  other arithmetic  21.1 us (5%)
  local copies, waits for them, and re-layouts  14.8 us (4%)
  between operations  14.8 us (4%)
    pallas_call x3, Pallas kernels, run_expert(): pl.pallas_call(functools.partial(expert_kernel, slots, kind, (len(blocks)...  68.6 us
    ppermute x48, starting transfers between devices, swap(): lax.ppermute(block, axis, [(i, i ^ rel) for i in range(lax.axis_size(axis...  51.5 us
    ppermute x48, waiting for transfers between devices, swap(): lax.ppermute(block, axis, [(i, i ^ rel) for i in range(lax.axis_size(axis...  43.2 us
    pallas_call x1, Pallas kernels, per_device(): pl.pallas_call(functools.partial(attn_backward_kernel, heads), in_specs=[...  28.6 us
    pallas_call x1, Pallas kernels, per_device(): pl.pallas_call(functools.partial(attn_forward_kernel, heads), in_specs=[S...  20.4 us
    pallas_call x1, Pallas kernels, run_first_grad(): pl.pallas_call(functools.partial(first_grad_kernel, len(rows)), grid_spec...  15.9 us
    pallas_call x1, Pallas kernels, run_second_grad(): pl.pallas_call(functools.partial(second_grad_kernel, len(acts)), grid=(4,...  15.7 us
    pallas_call x1, Pallas kernels, per_device(): pl.pallas_call(functools.partial(attn_prob_kernel, heads), in_specs=[SMEM...  14.3 us
  transfers between devices with their start and end apart: 54, of which 18 were waited for; matrix products, arithmetic and copies ran while one was open for 7% of the time, Pallas kernels for 57%

profile of v1, /device:TPU:0, one launch (start us, length us, event | category | flops | bytes accessed | tf_op | source)
XLA Modules:
  0.0 405.4 jit_solution(6630413343592973141)
XLA Ops:
  23.6 8.2 %shard_map.230.before_ref = bf16[1920,768]{1,0:T(8,128)(2,1)} custom-call(s32[1]{0:T(128)} %bitcast.1.me_ref, s32[2,640]{1,0:T(2,128)} %copy.72.places_ref, bf16[16,640]{1,0:T(8,128)(2,1)} %broadcast_bitcast_fusion.others_ref, bf16[640,768]{1,0:T(8,128)(2,1)} %refs_11_.1, bf16[192,640]{1,0:T(8,128)(2,1)} %get-tuple-element.190.refs_0_.w0), custom_call_target="tpu_custom_call" | custom-call | bytes 1024 | tf_op jit(solution)/shard_map/pallas_call | solution.py:1024
  31.7 5.8 %all-to-all-start.1 = ((bf16[8,240,768]{2,1,0:T(8,128)(2,1)}), bf16[8,240,768]{2,1,0:T(8,128)(2,1)S(1)}, u32[]{:S(2)}, u32[]{:S(2)}) async-start(bf16[8,240,768]{2,1,0:T(8,128)(2,1)} %bitcast.52), calls=%async_computation.1 | async-start | bytes 5898240 | tf_op jit(solution)/shard_map/all_to_all | solution.py:433
  45.8 10.6 %shard_map.231 = (bf16[4,640,768]{2,1,0:T(8,128)(2,1)}, bf16[2560,256]{1,0:T(8,128)(2,1)}, bf16[2560,256]{1,0:T(8,128)(2,1)}, bf16[2560,256]{1,0:T(8,128)(2,1)},...) custom-call(s32[1]{0:T(128)} %bitcast.me_ref, ...), custom_call_target="tpu_custom_call" | custom-call | bytes 1024 | tf_op jit(solution)/shard_map/pallas_call | solution.py:1041
  56.3 20.4 %shard_map.232 = (bf16[192,640]{1,0:T(8,128)(2,1)}, bf16[192,640]{1,0:T(8,128)(2,1)}, bf16[192,640]{1,0:T(8,128)(2,1)}, bf16[192,640]{1,0:T(8,128)(2,1)}, f32[256,2560]{1,0:T(8,128)}, /*index=5*/f32[160,384]{1,0:T(8,128)}) custom-call(s32[1]{0:T(128)} %bitcast.me_ref, s32[20]{0:T(128)} %bitcast.77, bf16[2560,256]{1,0:T(8,128)(2,1)} %get-tuple-element.195.q_ref, ...), custom_call_target="tpu_custom_call" | custom-call | flops 30400000000 | bytes 1024 | tf_op jit(solution)/shard_map/pallas_call | solution.py:1060
  82.1 4.8 %collective-permute-done.8.m2.refs_16_ = bf16[192,640]{1,0:T(8,128)(2,1)S(1)} collective-permute-done((bf16[192,640]{1,0:T(8,128)(2,1)}, bf16[192,640]{1,0:T(8,128)(2,1)S(1)}, u32[]{:S(2)}, u32[]{:S(2)}) %collective-permute-start.8) | collective-permute-done | bytes 245792 | tf_op jit(solution)/shard_map/ppermute | solution.py:439
  92.7 7.2 %shard_map.233 = (f32[640,768]{1,0:T(8,128)}, bf16[640,768]{1,0:T(8,128)(2,1)}, f32[640,2]{1,0:T(8,128)}, bf16[960,768]{1,0:T(8,128)(2,1)}, bf16[240,768]{1,0:T(...) custom-call(s32[2]{0:T(128)} %pad_add_fusion.me_ref, ...), custom_call_target="tpu_custom_call" | custom-call | bytes 1024 | tf_op jit(solution)/shard_map/pallas_call | solution.py:1079
  99.9 4.6 %all-to-all-done.1 = bf16[8,240,768]{2,1,0:T(8,128)(2,1)S(1)} async-done(((bf16[8,240,768]{2,1,0:T(8,128)(2,1)}), bf16[8,240,768]{2,1,0:T(8,128)(2,1)S(1)}, u32[]{:S(2)}, u32[]{:S(2)}) %all-to-all-start.1) | async-done | bytes 2949152 | tf_op jit(solution)/shard_map/all_to_all | solution.py:433
  104.5 4.3 %all-to-all-start = ((bf16[4,240,768]{2,1,0:T(8,128)(2,1)}), bf16[4,240,768]{2,1,0:T(8,128)(2,1)}, u32[]{:S(2)}, u32[]{:S(2)}) async-start(bf16[4,240,768]{2,1,0:T(8,128)(2,1)} %bitcast.57), calls=%async_computation | async-start | bytes 2949120 | tf_op jit(solution)/shard_map/all_to_all | solution.py:429
  108.9 14.3 %shard_map.234.refs_11_.refs_14_.prob_ref = bf16[10240,768]{1,0:T(8,128)(2,1)} custom-call(s32[20]{0:T(128)} %bitcast.78, bf16[2560,256]{1,0:T(8,128)(2,1)} %get-tuple-element.195.q_ref, bf16[2560,256]{1,0:T(8,128)(2,1)} %get-tuple-element.196.k_ref, f32[160,384]{1,0:T(8,128)} %get-tuple-element.224.lse_ref, f32[4,128,384]{2,1,0:T(8,128)} %get-tuple-element.200.bias_ref, ...), custom_call_target="tpu_custom_call" | custom-call | bytes 1024 | tf_op jit(solution)/shard_map/pallas_call | solution.py:1088
  131.2 12.7 %shard_map.235 = (bf16[1920,768]{1,0:T(8,128)(2,1)}, bf16[240,768]{1,0:T(8,128)(2,1)}, bf16[240,768]{1,0:T(8,128)(2,1)}, bf16[240,768]{1,0:T(8,128)(2,1)}, bf16[...) custom-call(s32[2]{0:T(128)} %pad_add_fusion.me_ref, bf16[960,768]{1,0:T(8,128)(2,1)} %get-tuple-element.228.refs_0_, ...), custom_call_target="tpu_custom_call" | custom-call | bytes 1024 | tf_op jit(solution)/shard_map/pallas_call | solution.py:689
  144.1 25.6 %shard_map.236 = (bf16[1920,768]{1,0:T(8,128)(2,1)}, bf16[960,768]{1,0:T(8,128)(2,1)}, bf16[720,768]{1,0:T(8,128)(2,1)}, bf16[720,768]{1,0:T(8,128)(2,1)}, bf16[...) custom-call(s32[2]{0:T(128)} %pad_add_fusion.me_ref, ...), custom_call_target="tpu_custom_call", output_to_operand_aliasing={{0}: (14, {})} | custom-call | bytes 1024 | tf_op jit(solution)/shard_map/pallas_call | solution.py:689
  169.7 4.5 %all-to-all-start.2 = ((bf16[4,240,768]{2,1,0:T(8,128)(2,1)}), bf16[4,240,768]{2,1,0:T(8,128)(2,1)}, u32[]{:S(2)}, u32[]{:S(2)}) async-start(bf16[4,240,768]{2,1,0:T(8,128)(2,1)} %bitcast.71), calls=%async_computation.2 | async-start | bytes 2949120 | tf_op jit(solution)/shard_map/all_to_all | solution.py:429
  176.2 30.3 %shard_map.237 = (bf16[1920,768]{1,0:T(8,128)(2,1)}, bf16[240,768]{1,0:T(8,128)(2,1)}, bf16[240,768]{1,0:T(8,128)(2,1)}, bf16[240,768]{1,0:T(8,128)(2,1)}, bf16[...) custom-call(s32[2]{0:T(128)} %pad_add_fusion.me_ref, ...), custom_call_target="tpu_custom_call", output_to_operand_aliasing={{0}: (16, {})} | custom-call | flops 1099511627776 | bytes 4294967296 | tf_op jit(solution)/shard_map/pallas_call | solution.py:689
  213.4 15.7 %shard_map.239 = (bf16[1536,768]{1,0:T(8,128)(2,1)}, bf16[1536,768]{1,0:T(8,128)(2,1)}) custom-call(bf16[240,3072]{1,0:T(8,128)(2,1)} %get-tuple-element.256.refs_0_, bf16[720,3072]{1,0:T(8,128)(2,1)} %get-tuple-element.257.refs_1_, bf16[960,3072]{1,0:T(8,128)(2,1)} %get-tuple-element.258.refs_2_, bf16[240,768]{1,0:T(8,128)(2,1)} %get-tuple-element.259.refs_3_, ...), custom_call_target="tpu_custom_call" | custom-call | bytes 1024 | tf_op jit(solution)/shard_map/pallas_call | solution.py:767
  229.1 15.9 %shard_map.238 = (bf16[384,3072]{1,0:T(8,128)(2,1)}, bf16[384,3072]{1,0:T(8,128)(2,1)}) custom-call(s32[2]{0:T(128)} %pad_add_fusion.me_ref, bf16[240,768]{1,0:T(8,128)(2,1)} %get-tuple-element.247.refs_0_, bf16[720,768]{1,0:T(8,128)(2,1)} %get-tuple-element.248.refs_1_, bf16[960,768]{1,0:T(8,128)(2,1)} %get-tuple-element.249.refs_2_, ...), custom_call_target="tpu_custom_call" | custom-call | bytes 1024 | tf_op jit(solution)/shard_map/pallas_call | solution.py:733
  246.1 5.1 %all-to-all-start.3 = ((bf16[8,240,768]{2,1,0:T(8,128)(2,1)}), bf16[8,240,768]{2,1,0:T(8,128)(2,1)S(1)}, u32[]{:S(2)}, u32[]{:S(2)}) async-start(bf16[8,240,768]{2,1,0:T(8,128)(2,1)} %bitcast.56), calls=%async_computation.3 | async-start | bytes 5898240 | tf_op jit(solution)/shard_map/all_to_all | solution.py:433
  251.3 13.0 %shard_map.240 = (f32[640,768]{1,0:T(8,128)}, bf16[192,640]{1,0:T(8,128)(2,1)}, bf16[192,640]{1,0:T(8,128)(2,1)}, bf16[192,640]{1,0:T(8,128)(2,1)}, bf16[192,640...) custom-call(s32[1]{0:T(128)} %bitcast.me_ref, bf16[960,768]{1,0:T(8,128)(2,1)} %bitcast.16.refs_6_.refs_0_, ...), custom_call_target="tpu_custom_call" | custom-call | bytes 1024 | tf_op jit(solution)/shard_map/pallas_call | solution.py:1123
  280.3 28.6 %shard_map.241 = (bf16[640,640]{1,0:T(8,128)(2,1)}, bf16[640,640]{1,0:T(8,128)(2,1)}, bf16[640,640]{1,0:T(8,128)(2,1)}, bf16[640,640]{1,0:T(8,128)(2,1)}, f32[16,384]{1,0:T(8,128)}) custom-call(s32[1]{0:T(128)} %bitcast.me_ref, s32[20]{0:T(128)} %bitcast.79, bf16[2560,256]{1,0:T(8,128)(2,1)} %get-tuple-element.195.q_ref, ...), custom_call_target="tpu_custom_call" | custom-call | flops 22000001024 | bytes 1024 | tf_op jit(solution)/shard_map/pallas_call | solution.py:1147
  309.7 8.4 %shard_map.242 = (bf16[288,640]{1,0:T(8,128)(2,1)}, bf16[288,640]{1,0:T(8,128)(2,1)}, bf16[256,640]{1,0:T(8,128)(2,1)}, bf16[256,640]{1,0:T(8,128)(2,1)}) custom-call(s32[1]{0:T(128)} %bitcast.1.me_ref, f32[16,384]{1,0:T(8,128)} %get-tuple-element.284.bins_ref, bf16[4,640,768]{2,1,0:T(8,128)(2,1)} %get-tuple-element.285.n_ref, ...), custom_call_target="tpu_custom_call" | custom-call | bytes 1024 | tf_op jit(solution)/shard_map/pallas_call | solution.py:1175
  323.8 4.5 %collective-permute-done.34 = bf16[256,640]{1,0:T(8,128)(2,1)S(1)} collective-permute-done((bf16[256,640]{1,0:T(8,128)(2,1)}, bf16[256,640]{1,0:T(8,128)(2,1)S(1)}, u32[]{:S(2)}, u32[]{:S(2)}) %collective-permute-start.34) | collective-permute-done | bytes 327712 | tf_op jit(solution)/shard_map/ppermute | solution.py:439
  342.2 6.4 %collective-permute-done.36.refs_3_ = bf16[64,640]{1,0:T(8,128)(2,1)S(1)} collective-permute-done((bf16[64,640]{1,0:T(8,128)(2,1)S(1)}, bf16[64,640]{1,0:T(8,128)(2,1)S(1)}, u32[]{:S(2)}, u32[]{:S(2)}) %collective-permute-start.36) | collective-permute-done | bytes 81952 | tf_op jit(solution)/shard_map/ppermute | solution.py:439
  352.9 5.4 %collective-permute-done.42.d3 = bf16[640,640]{1,0:T(8,128)(2,1)} collective-permute-done((bf16[640,640]{1,0:T(8,128)(2,1)}, bf16[640,640]{1,0:T(8,128)(2,1)}, u32[]{:S(2)}, u32[]{:S(2)}) %collective-permute-start.42) | collective-permute-done | bytes 819232 | tf_op jit(solution)/shard_map/ppermute | solution.py:439
  370.7 6.6 %shard_map.245 = bf16[640,768]{1,0:T(8,128)(2,1)} custom-call(s32[1]{0:T(128)} %bitcast.1.me_ref, bf16[1920,768]{1,0:T(8,128)(2,1)} %bitcast.55, s32[640,2]{1,0:T(8,128)} %copy-done.3, f32[640,768]{1,0:T(8,128)} %get-tuple-element.225.before_ref.refs_8_.after_ref), custom_call_target="tpu_custom_call" | custom-call | bytes 1024 | tf_op jit(solution)/shard_map/pallas_call | solution.py:1216
  380.9 8.8 %shard_map.246 = bf16[640,768]{1,0:T(8,128)(2,1)} custom-call(s32[1]{0:T(128)} %bitcast.me_ref, bf16[640,768]{1,0:T(8,128)(2,1)} %x_ref.3, f32[1,768]{1,0:T(1,128)} %get-tuple-element.333.gain_ref, f32[640,768]{1,0:T(8,128)} %get-tuple-element.334.after_ref, bf16[640,640]{1,0:T(8,128)(2,1)} %get-tuple-element.335.d0, ...), custom_call_target="tpu_custom_call" | custom-call | bytes 1024 | tf_op jit(solution)/shard_map/pallas_call | solution.py:1230
  (216 shorter events, 119.0 us)
Async XLA Ops:
  7.2 34.9 %collective-permute-start = (bf16[640,768]{1,0:T(8,128)(2,1)}, bf16[640,768]{1,0:T(8,128)(2,1)}, u32[]{:S(2)}, u32[]{:S(2)}) collective-permute-start(bf16[640,768]{1,0:T(8,128)(2,1)} %x_ref.3), channel_id=1, source_target_pairs={{0,2},{1,3},{2,0},{3,1},{4,6},{5,7},{6,4},{7,5},{8,10},{9,11},{10,... | collective-permute-start | bytes 2949128 | tf_op jit(solution)/shard_map/ppermute | solution.py:439
  31.7 72.8 %all-to-all-start.1 = ((bf16[8,240,768]{2,1,0:T(8,128)(2,1)}), bf16[8,240,768]{2,1,0:T(8,128)(2,1)S(1)}, u32[]{:S(2)}, u32[]{:S(2)}) async-start(bf16[8,240,768]{2,1,0:T(8,128)(2,1)} %bitcast.52), calls=%async_computation.1 | async-start | bytes 5898240 | tf_op jit(solution)/shard_map/all_to_all | solution.py:433
  37.6 39.7 %all-gather.5.cloned.1.call-start = ((), (), s32[]{:S(2)}) async-start(), calls=%async_computation.4 | async-start | bytes 1474560 | tf_op jit(solution)/shard_map/all_gather | solution.py:1070
  42.8 34.5 %collective-permute-start.6 = (bf16[192,3072]{1,0:T(8,128)(2,1)}, bf16[192,3072]{1,0:T(8,128)(2,1)}, u32[]{:S(2)}, u32[]{:S(2)}) collective-permute-start(bf16[192,3072]{1,0:T(8,128)(2,1)} %bitcast.59), channel_id=1, source_target_pairs={{0,2},{1,3},{2,0},{3,1},{4,6},{5,7},{6,4},{7,5},{8,10},{9,11},{10,... | collective-permute-start | bytes 3538952 | tf_op jit(solution)/shard_map/ppermute | solution.py:439
  44.6 48.1 %collective-permute-start.10 = (bf16[192,3072]{1,0:T(8,128)(2,1)}, bf16[192,3072]{1,0:T(8,128)(2,1)}, u32[]{:S(2)}, u32[]{:S(2)}) collective-permute-start(bf16[192,3072]{1,0:T(8,128)(2,1)} %bitcast.60), channel_id=1, source_target_pairs={{0,1},{1,0},{2,3},{3,2},{4,5},{5,4},{6,7},{7,6},{8,9},{9,8},{10,11... | collective-permute-start | bytes 3538952 | tf_op jit(solution)/shard_map/ppermute | solution.py:439
  44.6 48.1 %collective-permute-start.12 = (bf16[768,768]{1,0:T(8,128)(2,1)}, bf16[768,768]{1,0:T(8,128)(2,1)}, u32[]{:S(2)}, u32[]{:S(2)}) collective-permute-start(bf16[768,768]{1,0:T(8,128)(2,1)} %bitcast.64), channel_id=1, source_target_pairs={{0,1},{1,0},{2,3},{3,2},{4,5},{5,4},{6,7},{7,6},{8,9},{9,8},{10,11... | collective-permute-start | bytes 3538952 | tf_op jit(solution)/shard_map/ppermute | solution.py:439
  90.5 32.6 %collective-permute-start.13 = (bf16[768,768]{1,0:T(8,128)(2,1)}, bf16[768,768]{1,0:T(8,128)(2,1)}, u32[]{:S(2)}, u32[]{:S(2)}) collective-permute-start(bf16[768,768]{1,0:T(8,128)(2,1)} %bitcast.65), channel_id=1, source_target_pairs={{0,2},{1,3},{2,0},{3,1},{4,6},{5,7},{6,4},{7,5},{8,10},{9,11},{10,... | collective-permute-start | bytes 3538952 | tf_op jit(solution)/shard_map/ppermute | solution.py:439
  104.5 39.6 %all-to-all-start = ((bf16[4,240,768]{2,1,0:T(8,128)(2,1)}), bf16[4,240,768]{2,1,0:T(8,128)(2,1)}, u32[]{:S(2)}, u32[]{:S(2)}) async-start(bf16[4,240,768]{2,1,0:T(8,128)(2,1)} %bitcast.57), calls=%async_computation | async-start | bytes 2949120 | tf_op jit(solution)/shard_map/all_to_all | solution.py:429
  108.9 120.2 %all-gather.7.cloned.1.call-start = ((), (), s32[]{:S(2)}) async-start(), calls=%async_computation.5 | async-start | bytes 4915200 | tf_op jit(solution)/shard_map/all_gather | solution.py:1116
  123.3 50.9 %collective-permute-start.15 = (bf16[240,768]{1,0:T(8,128)(2,1)}, bf16[240,768]{1,0:T(8,128)(2,1)S(1)}, u32[]{:S(2)}, u32[]{:S(2)}) collective-permute-start(bf16[240,768]{1,0:T(8,128)(2,1)} %get-tuple-element.238), channel_id=1, source_target_pairs={{0,8},{4,12},{8,0},{12,4},{16,24},{20,28},{24,16},{28,20},{1,9},{5... | collective-permute-start | bytes 1105928 | tf_op jit(solution)/shard_map/ppermute | solution.py:439
  123.3 51.9 %collective-permute-start.16 = (bf16[240,768]{1,0:T(8,128)(2,1)}, bf16[240,768]{1,0:T(8,128)(2,1)S(1)}, u32[]{:S(2)}, u32[]{:S(2)}) collective-permute-start(bf16[240,768]{1,0:T(8,128)(2,1)} %get-tuple-element.239), channel_id=1, source_target_pairs={{0,12},{4,8},{8,4},{12,0},{16,28},{20,24},{24,20},{28,16},{1,13},{... | collective-permute-start | bytes 1105928 | tf_op jit(solution)/shard_map/ppermute | solution.py:439
  126.7 48.5 %collective-permute-start.17 = (bf16[240,768]{1,0:T(8,128)(2,1)}, bf16[240,768]{1,0:T(8,128)(2,1)S(1)}, u32[]{:S(2)}, u32[]{:S(2)}) collective-permute-start(bf16[240,768]{1,0:T(8,128)(2,1)} %get-tuple-element.240), channel_id=1, source_target_pairs={{0,24},{4,28},{8,16},{12,20},{16,8},{20,12},{24,0},{28,4},{1,25},{... | collective-permute-start | bytes 1105928 | tf_op jit(solution)/shard_map/ppermute | solution.py:439
  128.6 46.6 %collective-permute-start.18 = (bf16[240,768]{1,0:T(8,128)(2,1)S(1)}, bf16[240,768]{1,0:T(8,128)(2,1)S(1)}, u32[]{:S(2)}, u32[]{:S(2)}) collective-permute-start(bf16[240,768]{1,0:T(8,128)(2,1)S(1)} %copy-done.26), channel_id=1, source_target_pairs={{0,28},{4,24},{8,20},{12,16},{16,12},{20,8},{24,4},{28,0},{1,29},{... | collective-permute-start | bytes 1105928 | tf_op jit(solution)/shard_map/ppermute | solution.py:439
  169.7 59.4 %all-to-all-start.2 = ((bf16[4,240,768]{2,1,0:T(8,128)(2,1)}), bf16[4,240,768]{2,1,0:T(8,128)(2,1)}, u32[]{:S(2)}, u32[]{:S(2)}) async-start(bf16[4,240,768]{2,1,0:T(8,128)(2,1)} %bitcast.71), calls=%async_computation.2 | async-start | bytes 2949120 | tf_op jit(solution)/shard_map/all_to_all | solution.py:429
  206.5 38.5 %collective-permute-start.19 = (bf16[240,768]{1,0:T(8,128)(2,1)}, bf16[240,768]{1,0:T(8,128)(2,1)S(1)}, u32[]{:S(2)}, u32[]{:S(2)}) collective-permute-start(bf16[240,768]{1,0:T(8,128)(2,1)} %get-tuple-element.243), channel_id=1, source_target_pairs={{0,8},{4,12},{8,0},{12,4},{16,24},{20,28},{24,16},{28,20},{1,9},{5... | collective-permute-start | bytes 1105928 | tf_op jit(solution)/shard_map/ppermute | solution.py:439
  207.4 37.6 %collective-permute-start.20 = (bf16[240,768]{1,0:T(8,128)(2,1)}, bf16[240,768]{1,0:T(8,128)(2,1)S(1)}, u32[]{:S(2)}, u32[]{:S(2)}) collective-permute-start(bf16[240,768]{1,0:T(8,128)(2,1)} %get-tuple-element.244), channel_id=1, source_target_pairs={{0,12},{4,8},{8,4},{12,0},{16,28},{20,24},{24,20},{28,16},{1,13},{... | collective-permute-start | bytes 1105928 | tf_op jit(solution)/shard_map/ppermute | solution.py:439
  209.2 35.9 %collective-permute-start.21 = (bf16[240,768]{1,0:T(8,128)(2,1)}, bf16[240,768]{1,0:T(8,128)(2,1)S(1)}, u32[]{:S(2)}, u32[]{:S(2)}) collective-permute-start(bf16[240,768]{1,0:T(8,128)(2,1)} %get-tuple-element.245), channel_id=1, source_target_pairs={{0,24},{4,28},{8,16},{12,20},{16,8},{20,12},{24,0},{28,4},{1,25},{... | collective-permute-start | bytes 1105928 | tf_op jit(solution)/shard_map/ppermute | solution.py:439
  211.6 33.5 %collective-permute-start.22 = (bf16[240,768]{1,0:T(8,128)(2,1)}, bf16[240,768]{1,0:T(8,128)(2,1)S(1)}, u32[]{:S(2)}, u32[]{:S(2)}) collective-permute-start(bf16[240,768]{1,0:T(8,128)(2,1)} %get-tuple-element.246), channel_id=1, source_target_pairs={{0,28},{4,24},{8,20},{12,16},{16,12},{20,8},{24,4},{28,0},{1,29},{... | collective-permute-start | bytes 1105928 | tf_op jit(solution)/shard_map/ppermute | solution.py:439
  246.1 71.9 %all-to-all-start.3 = ((bf16[8,240,768]{2,1,0:T(8,128)(2,1)}), bf16[8,240,768]{2,1,0:T(8,128)(2,1)S(1)}, u32[]{:S(2)}, u32[]{:S(2)}) async-start(bf16[8,240,768]{2,1,0:T(8,128)(2,1)} %bitcast.56), calls=%async_computation.3 | async-start | bytes 5898240 | tf_op jit(solution)/shard_map/all_to_all | solution.py:433
  278.3 30.7 %collective-permute-start.29 = (bf16[192,896]{1,0:T(8,128)(2,1)S(1)}, bf16[192,896]{1,0:T(8,128)(2,1)S(1)}, u32[]{:S(2)}, u32[]{:S(2)}) collective-permute-start(bf16[192,896]{1,0:T(8,128)(2,1)S(1)} %add_convert_fusion.3), channel_id=1, source_target_pairs={{0,2},{1,3},{2,0},{3,1},{4,6},{5,7},{6,4},{7,5},{8,10},{9,11},{10,... | collective-permute-start | bytes 1032200 | tf_op jit(solution)/shard_map/ppermute | solution.py:439
  278.9 39.1 %collective-permute-start.30 = (bf16[768,768]{1,0:T(8,128)(2,1)}, bf16[768,768]{1,0:T(8,128)(2,1)}, u32[]{:S(2)}, u32[]{:S(2)}) collective-permute-start(bf16[768,768]{1,0:T(8,128)(2,1)} %add_convert_fusion.1), channel_id=1, source_target_pairs={{0,2},{1,3},{2,0},{3,1},{4,6},{5,7},{6,4},{7,5},{8,10},{9,11},{10,... | collective-permute-start | bytes 3538952 | tf_op jit(solution)/shard_map/ppermute | solution.py:439
  322.3 30.6 %collective-permute-start.41 = (bf16[640,640]{1,0:T(8,128)(2,1)}, bf16[640,640]{1,0:T(8,128)(2,1)}, u32[]{:S(2)}, u32[]{:S(2)}) collective-permute-start(bf16[640,640]{1,0:T(8,128)(2,1)} %get-tuple-element.287.d1), channel_id=1, source_target_pairs={{0,1},{1,0},{2,3},{3,2},{4,5},{5,4},{6,7},{7,6},{8,9},{9,8},{10,11... | collective-permute-start | bytes 2457608 | tf_op jit(solution)/shard_map/ppermute | solution.py:439
  322.3 35.9 %collective-permute-start.42 = (bf16[640,640]{1,0:T(8,128)(2,1)}, bf16[640,640]{1,0:T(8,128)(2,1)}, u32[]{:S(2)}, u32[]{:S(2)}) collective-permute-start(bf16[640,640]{1,0:T(8,128)(2,1)} %get-tuple-element.289.d3), channel_id=1, source_target_pairs={{0,3},{1,2},{2,1},{3,0},{4,7},{5,6},{6,5},{7,4},{8,11},{9,10},{10,... | collective-permute-start | bytes 2457608 | tf_op jit(solution)/shard_map/ppermute | solution.py:439
  360.0 29.7 %collective-permute-start.47 = (bf16[192,3072]{1,0:T(8,128)(2,1)}, bf16[192,3072]{1,0:T(8,128)(2,1)S(1)}, u32[]{:S(2)}, u32[]{:S(2)}) collective-permute-start(bf16[192,3072]{1,0:T(8,128)(2,1)} %add_convert_fusion), channel_id=1, source_target_pairs={{0,2},{1,3},{2,0},{3,1},{4,6},{5,7},{6,4},{7,5},{8,10},{9,11},{10,... | collective-permute-start | bytes 3538952 | tf_op jit(solution)/shard_map/ppermute | solution.py:439
  (65 other events, 633.3 us)
Sparse Core Ops, SparseCore 0:
  44.7 24.3 all-gather.4
  144.0 31.9 all-gather.6

commit v2 on v1

--- a/solution.py
+++ b/solution.py
@@ -496,7 +496,7 @@
         out_ref[pl.ds(pl.multiple_of(expert * count, 16), count), :] = picked.astype(BF16)
         return carry
 
-    lax.fori_loop(0, slots.n_expert, one, 0)
+    lax.fori_loop(0, slots.n_expert, one, 0, unroll=2)
 
 
 def post_kernel(
@@ -846,7 +846,7 @@
         branch_ref[at, :] = branch
         return carry
 
-    lax.fori_loop(0, tokens // part, one, 0)
+    lax.fori_loop(0, tokens // part, one, 0, unroll=2)
     for rel, mixed_ref in enumerate(mixed_refs):
         mixed_ref[...] = dot(w_ref[jnp.bitwise_xor(me_ref[0], rel)], branch_ref[...], NT).astype(BF16)
     width = branch_ref.shape[1]
@@ -877,7 +877,7 @@
         out_ref[at, :] = total.astype(BF16)
         return carry
 
-    lax.fori_loop(0, after_ref.shape[0] // part, one, 0)
+    lax.fori_loop(0, after_ref.shape[0] // part, one, 0, unroll=2)
 
 
 def final_kernel(me_ref, x_ref, gain_ref, after_ref, d0, d1, d2, d3, w_ref, out_ref):

time: 409 us -> 406 us (level)
  transfers between devices with their start and end apart: 54 -> 54, of which waited for: 18 -> 19; matrix products, arithmetic and copies ran while one was open for 7% -> 7% of each run, Pallas kernels for 57% -> 57%
where the time goes in v2:
time: 406 us; the launch traced here: 402 us
  Pallas kernels  232 us (57%)
  starting transfers between devices  71.1 us (18%)
  waiting for transfers between devices  48.6 us (12%)
  other arithmetic  21.1 us (5%)
  between operations  14.8 us (4%)
  local copies, waits for them, and re-layouts  14.3 us (4%)
    pallas_call x3, Pallas kernels, run_expert(): pl.pallas_call(functools.partial(expert_kernel, slots, kind, (len(blocks)...  68.6 us
    ppermute x48, starting transfers between devices, swap(): lax.ppermute(block, axis, [(i, i ^ rel) for i in range(lax.axis_size(axis...  51.2 us
    ppermute x48, waiting for transfers between devices, swap(): lax.ppermute(block, axis, [(i, i ^ rel) for i in range(lax.axis_size(axis...  43.4 us
    pallas_call x1, Pallas kernels, per_device(): pl.pallas_call(functools.partial(attn_backward_kernel, heads), in_specs=[...  28.5 us
    pallas_call x1, Pallas kernels, per_device(): pl.pallas_call(functools.partial(attn_forward_kernel, heads), in_specs=[S...  20.2 us
    pallas_call x1, Pallas kernels, run_first_grad(): pl.pallas_call(functools.partial(first_grad_kernel, len(rows)), grid_spec...  16.4 us
    pallas_call x1, Pallas kernels, run_second_grad(): pl.pallas_call(functools.partial(second_grad_kernel, len(acts)), grid=(4,...  15.7 us
    pallas_call x1, Pallas kernels, per_device(): pl.pallas_call(functools.partial(attn_prob_kernel, heads), in_specs=[SMEM...  13.9 us
  transfers between devices with their start and end apart: 54, of which 19 were waited for; matrix products, arithmetic and copies ran while one was open for 7% of the time, Pallas kernels for 57%

profile of v2, /device:TPU:0, one launch (start us, length us, event | category | flops | bytes accessed | tf_op | source)
XLA Modules:
  0.0 401.8 jit_solution(4421166156110682497)
XLA Ops:
  23.6 7.1 %shard_map.230.before_ref = bf16[1920,768]{1,0:T(8,128)(2,1)} custom-call(s32[1]{0:T(128)} %bitcast.1.me_ref, s32[2,640]{1,0:T(2,128)} %copy.72.places_ref, bf16[16,640]{1,0:T(8,128)(2,1)} %broadcast_bitcast_fusion.others_ref, bf16[640,768]{1,0:T(8,128)(2,1)} %refs_11_.1, bf16[192,640]{1,0:T(8,128)(2,1)} %get-tuple-element.190.refs_0_.w0), custom_call_target="tpu_custom_call" | custom-call | bytes 1024 | tf_op jit(solution)/shard_map/pallas_call | solution.py:1024
  30.6 5.8 %all-to-all-start.1 = ((bf16[8,240,768]{2,1,0:T(8,128)(2,1)}), bf16[8,240,768]{2,1,0:T(8,128)(2,1)S(1)}, u32[]{:S(2)}, u32[]{:S(2)}) async-start(bf16[8,240,768]{2,1,0:T(8,128)(2,1)} %bitcast.52), calls=%async_computation.1 | async-start | bytes 5898240 | tf_op jit(solution)/shard_map/all_to_all | solution.py:433
  38.3 3.8 collective-permute-done.3.w3
  45.8 10.6 %shard_map.231 = (bf16[4,640,768]{2,1,0:T(8,128)(2,1)}, bf16[2560,256]{1,0:T(8,128)(2,1)}, bf16[2560,256]{1,0:T(8,128)(2,1)}, bf16[2560,256]{1,0:T(8,128)(2,1)},...) custom-call(s32[1]{0:T(128)} %bitcast.me_ref, ...), custom_call_target="tpu_custom_call" | custom-call | bytes 1024 | tf_op jit(solution)/shard_map/pallas_call | solution.py:1041
  56.3 20.2 %shard_map.232 = (bf16[192,640]{1,0:T(8,128)(2,1)}, bf16[192,640]{1,0:T(8,128)(2,1)}, bf16[192,640]{1,0:T(8,128)(2,1)}, bf16[192,640]{1,0:T(8,128)(2,1)}, f32[256,2560]{1,0:T(8,128)}, /*index=5*/f32[160,384]{1,0:T(8,128)}) custom-call(s32[1]{0:T(128)} %bitcast.me_ref, s32[20]{0:T(128)} %bitcast.77, bf16[2560,256]{1,0:T(8,128)(2,1)} %get-tuple-element.195.q_ref, ...), custom_call_target="tpu_custom_call" | custom-call | flops 30400000000 | bytes 1024 | tf_op jit(solution)/shard_map/pallas_call | solution.py:1060
  82.1 4.8 %collective-permute-done.8.m2.refs_16_ = bf16[192,640]{1,0:T(8,128)(2,1)S(1)} collective-permute-done((bf16[192,640]{1,0:T(8,128)(2,1)}, bf16[192,640]{1,0:T(8,128)(2,1)S(1)}, u32[]{:S(2)}, u32[]{:S(2)}) %collective-permute-start.8) | collective-permute-done | bytes 245792 | tf_op jit(solution)/shard_map/ppermute | solution.py:439
  92.7 7.2 %shard_map.233 = (f32[640,768]{1,0:T(8,128)}, bf16[640,768]{1,0:T(8,128)(2,1)}, f32[640,2]{1,0:T(8,128)}, bf16[960,768]{1,0:T(8,128)(2,1)}, bf16[240,768]{1,0:T(...) custom-call(s32[2]{0:T(128)} %pad_add_fusion.me_ref, ...), custom_call_target="tpu_custom_call" | custom-call | bytes 1024 | tf_op jit(solution)/shard_map/pallas_call | solution.py:1079
  103.4 4.3 %all-to-all-start = ((bf16[4,240,768]{2,1,0:T(8,128)(2,1)}), bf16[4,240,768]{2,1,0:T(8,128)(2,1)}, u32[]{:S(2)}, u32[]{:S(2)}) async-start(bf16[4,240,768]{2,1,0:T(8,128)(2,1)} %bitcast.57), calls=%async_computation | async-start | bytes 2949120 | tf_op jit(solution)/shard_map/all_to_all | solution.py:429
  107.8 13.9 %shard_map.234.refs_11_.refs_14_.prob_ref = bf16[10240,768]{1,0:T(8,128)(2,1)} custom-call(s32[20]{0:T(128)} %bitcast.78, bf16[2560,256]{1,0:T(8,128)(2,1)} %get-tuple-element.195.q_ref, bf16[2560,256]{1,0:T(8,128)(2,1)} %get-tuple-element.196.k_ref, f32[160,384]{1,0:T(8,128)} %get-tuple-element.224.lse_ref, f32[4,128,384]{2,1,0:T(8,128)} %get-tuple-element.200.bias_ref, ...), custom_call_target="tpu_custom_call" | custom-call | bytes 1024 | tf_op jit(solution)/shard_map/pallas_call | solution.py:1088
  129.7 12.7 %shard_map.235 = (bf16[1920,768]{1,0:T(8,128)(2,1)}, bf16[240,768]{1,0:T(8,128)(2,1)}, bf16[240,768]{1,0:T(8,128)(2,1)}, bf16[240,768]{1,0:T(8,128)(2,1)}, bf16[...) custom-call(s32[2]{0:T(128)} %pad_add_fusion.me_ref, bf16[960,768]{1,0:T(8,128)(2,1)} %get-tuple-element.228.refs_0_, ...), custom_call_target="tpu_custom_call" | custom-call | bytes 1024 | tf_op jit(solution)/shard_map/pallas_call | solution.py:689
  143.2 25.6 %shard_map.236 = (bf16[1920,768]{1,0:T(8,128)(2,1)}, bf16[960,768]{1,0:T(8,128)(2,1)}, bf16[720,768]{1,0:T(8,128)(2,1)}, bf16[720,768]{1,0:T(8,128)(2,1)}, bf16[...) custom-call(s32[2]{0:T(128)} %pad_add_fusion.me_ref, ...), custom_call_target="tpu_custom_call", output_to_operand_aliasing={{0}: (14, {})} | custom-call | bytes 1024 | tf_op jit(solution)/shard_map/pallas_call | solution.py:689
  168.8 4.6 %all-to-all-start.2 = ((bf16[4,240,768]{2,1,0:T(8,128)(2,1)}), bf16[4,240,768]{2,1,0:T(8,128)(2,1)}, u32[]{:S(2)}, u32[]{:S(2)}) async-start(bf16[4,240,768]{2,1,0:T(8,128)(2,1)} %bitcast.71), calls=%async_computation.2 | async-start | bytes 2949120 | tf_op jit(solution)/shard_map/all_to_all | solution.py:429
  174.7 30.3 %shard_map.237 = (bf16[1920,768]{1,0:T(8,128)(2,1)}, bf16[240,768]{1,0:T(8,128)(2,1)}, bf16[240,768]{1,0:T(8,128)(2,1)}, bf16[240,768]{1,0:T(8,128)(2,1)}, bf16[...) custom-call(s32[2]{0:T(128)} %pad_add_fusion.me_ref, ...), custom_call_target="tpu_custom_call", output_to_operand_aliasing={{0}: (16, {})} | custom-call | flops 1099511627776 | bytes 4294967296 | tf_op jit(solution)/shard_map/pallas_call | solution.py:689
  211.9 15.7 %shard_map.239 = (bf16[1536,768]{1,0:T(8,128)(2,1)}, bf16[1536,768]{1,0:T(8,128)(2,1)}) custom-call(bf16[240,3072]{1,0:T(8,128)(2,1)} %get-tuple-element.256.refs_0_, bf16[720,3072]{1,0:T(8,128)(2,1)} %get-tuple-element.257.refs_1_, bf16[960,3072]{1,0:T(8,128)(2,1)} %get-tuple-element.258.refs_2_, bf16[240,768]{1,0:T(8,128)(2,1)} %get-tuple-element.259.refs_3_, ...), custom_call_target="tpu_custom_call" | custom-call | bytes 1024 | tf_op jit(solution)/shard_map/pallas_call | solution.py:767
  227.6 16.4 %shard_map.238 = (bf16[384,3072]{1,0:T(8,128)(2,1)}, bf16[384,3072]{1,0:T(8,128)(2,1)}) custom-call(s32[2]{0:T(128)} %pad_add_fusion.me_ref, bf16[240,768]{1,0:T(8,128)(2,1)} %get-tuple-element.247.refs_0_, bf16[720,768]{1,0:T(8,128)(2,1)} %get-tuple-element.248.refs_1_, bf16[960,768]{1,0:T(8,128)(2,1)} %get-tuple-element.249.refs_2_, ...), custom_call_target="tpu_custom_call" | custom-call | bytes 1024 | tf_op jit(solution)/shard_map/pallas_call | solution.py:733
  245.1 4.5 %all-to-all-start.3 = ((bf16[8,240,768]{2,1,0:T(8,128)(2,1)}), bf16[8,240,768]{2,1,0:T(8,128)(2,1)S(1)}, u32[]{:S(2)}, u32[]{:S(2)}) async-start(bf16[8,240,768]{2,1,0:T(8,128)(2,1)} %bitcast.56), calls=%async_computation.3 | async-start | bytes 5898240 | tf_op jit(solution)/shard_map/all_to_all | solution.py:433
  249.7 12.0 %shard_map.240 = (f32[640,768]{1,0:T(8,128)}, bf16[192,640]{1,0:T(8,128)(2,1)}, bf16[192,640]{1,0:T(8,128)(2,1)}, bf16[192,640]{1,0:T(8,128)(2,1)}, bf16[192,640...) custom-call(s32[1]{0:T(128)} %bitcast.me_ref, bf16[960,768]{1,0:T(8,128)(2,1)} %bitcast.16.refs_6_.refs_0_, ...), custom_call_target="tpu_custom_call" | custom-call | bytes 1024 | tf_op jit(solution)/shard_map/pallas_call | solution.py:1123
  277.6 28.5 %shard_map.241 = (bf16[640,640]{1,0:T(8,128)(2,1)}, bf16[640,640]{1,0:T(8,128)(2,1)}, bf16[640,640]{1,0:T(8,128)(2,1)}, bf16[640,640]{1,0:T(8,128)(2,1)}, f32[16,384]{1,0:T(8,128)}) custom-call(s32[1]{0:T(128)} %bitcast.me_ref, s32[20]{0:T(128)} %bitcast.79, bf16[2560,256]{1,0:T(8,128)(2,1)} %get-tuple-element.195.q_ref, ...), custom_call_target="tpu_custom_call" | custom-call | flops 22000001024 | bytes 1024 | tf_op jit(solution)/shard_map/pallas_call | solution.py:1147
  306.8 8.4 %shard_map.242 = (bf16[288,640]{1,0:T(8,128)(2,1)}, bf16[288,640]{1,0:T(8,128)(2,1)}, bf16[256,640]{1,0:T(8,128)(2,1)}, bf16[256,640]{1,0:T(8,128)(2,1)}) custom-call(s32[1]{0:T(128)} %bitcast.1.me_ref, f32[16,384]{1,0:T(8,128)} %get-tuple-element.284.bins_ref, bf16[4,640,768]{2,1,0:T(8,128)(2,1)} %get-tuple-element.285.n_ref, ...), custom_call_target="tpu_custom_call" | custom-call | bytes 1024 | tf_op jit(solution)/shard_map/pallas_call | solution.py:1175
  320.9 4.5 %collective-permute-done.34 = bf16[256,640]{1,0:T(8,128)(2,1)S(1)} collective-permute-done((bf16[256,640]{1,0:T(8,128)(2,1)}, bf16[256,640]{1,0:T(8,128)(2,1)S(1)}, u32[]{:S(2)}, u32[]{:S(2)}) %collective-permute-start.34) | collective-permute-done | bytes 327712 | tf_op jit(solution)/shard_map/ppermute | solution.py:439
  339.3 6.4 %collective-permute-done.36.refs_3_ = bf16[64,640]{1,0:T(8,128)(2,1)S(1)} collective-permute-done((bf16[64,640]{1,0:T(8,128)(2,1)S(1)}, bf16[64,640]{1,0:T(8,128)(2,1)S(1)}, u32[]{:S(2)}, u32[]{:S(2)}) %collective-permute-start.36) | collective-permute-done | bytes 81952 | tf_op jit(solution)/shard_map/ppermute | solution.py:439
  350.1 5.3 %collective-permute-done.42.d3 = bf16[640,640]{1,0:T(8,128)(2,1)} collective-permute-done((bf16[640,640]{1,0:T(8,128)(2,1)}, bf16[640,640]{1,0:T(8,128)(2,1)}, u32[]{:S(2)}, u32[]{:S(2)}) %collective-permute-start.42) | collective-permute-done | bytes 819232 | tf_op jit(solution)/shard_map/ppermute | solution.py:439
  367.8 5.8 %shard_map.245 = bf16[640,768]{1,0:T(8,128)(2,1)} custom-call(s32[1]{0:T(128)} %bitcast.1.me_ref, bf16[1920,768]{1,0:T(8,128)(2,1)} %bitcast.55, s32[640,2]{1,0:T(8,128)} %copy-done.3, f32[640,768]{1,0:T(8,128)} %get-tuple-element.225.before_ref.refs_8_.after_ref), custom_call_target="tpu_custom_call" | custom-call | bytes 1024 | tf_op jit(solution)/shard_map/pallas_call | solution.py:1216
  377.3 8.8 %shard_map.246 = bf16[640,768]{1,0:T(8,128)(2,1)} custom-call(s32[1]{0:T(128)} %bitcast.me_ref, bf16[640,768]{1,0:T(8,128)(2,1)} %x_ref.3, f32[1,768]{1,0:T(1,128)} %get-tuple-element.333.gain_ref, f32[640,768]{1,0:T(8,128)} %get-tuple-element.334.after_ref, bf16[640,640]{1,0:T(8,128)(2,1)} %get-tuple-element.335.d0, ...), custom_call_target="tpu_custom_call" | custom-call | bytes 1024 | tf_op jit(solution)/shard_map/pallas_call | solution.py:1230
  (216 shorter events, 119.8 us)
Async XLA Ops:
  7.2 34.9 %collective-permute-start = (bf16[640,768]{1,0:T(8,128)(2,1)}, bf16[640,768]{1,0:T(8,128)(2,1)}, u32[]{:S(2)}, u32[]{:S(2)}) collective-permute-start(bf16[640,768]{1,0:T(8,128)(2,1)} %x_ref.3), channel_id=1, source_target_pairs={{0,2},{1,3},{2,0},{3,1},{4,6},{5,7},{6,4},{7,5},{8,10},{9,11},{10,... | collective-permute-start | bytes 2949128 | tf_op jit(solution)/shard_map/ppermute | solution.py:439
  30.6 72.8 %all-to-all-start.1 = ((bf16[8,240,768]{2,1,0:T(8,128)(2,1)}), bf16[8,240,768]{2,1,0:T(8,128)(2,1)S(1)}, u32[]{:S(2)}, u32[]{:S(2)}) async-start(bf16[8,240,768]{2,1,0:T(8,128)(2,1)} %bitcast.52), calls=%async_computation.1 | async-start | bytes 5898240 | tf_op jit(solution)/shard_map/all_to_all | solution.py:433
  36.5 40.8 %all-gather.5.cloned.1.call-start = ((), (), s32[]{:S(2)}) async-start(), calls=%async_computation.4 | async-start | bytes 1474560 | tf_op jit(solution)/shard_map/all_gather | solution.py:1070
  42.8 34.5 %collective-permute-start.6 = (bf16[192,3072]{1,0:T(8,128)(2,1)}, bf16[192,3072]{1,0:T(8,128)(2,1)}, u32[]{:S(2)}, u32[]{:S(2)}) collective-permute-start(bf16[192,3072]{1,0:T(8,128)(2,1)} %bitcast.59), channel_id=1, source_target_pairs={{0,2},{1,3},{2,0},{3,1},{4,6},{5,7},{6,4},{7,5},{8,10},{9,11},{10,... | collective-permute-start | bytes 3538952 | tf_op jit(solution)/shard_map/ppermute | solution.py:439
  44.6 48.1 %collective-permute-start.10 = (bf16[192,3072]{1,0:T(8,128)(2,1)}, bf16[192,3072]{1,0:T(8,128)(2,1)}, u32[]{:S(2)}, u32[]{:S(2)}) collective-permute-start(bf16[192,3072]{1,0:T(8,128)(2,1)} %bitcast.60), channel_id=1, source_target_pairs={{0,1},{1,0},{2,3},{3,2},{4,5},{5,4},{6,7},{7,6},{8,9},{9,8},{10,11... | collective-permute-start | bytes 3538952 | tf_op jit(solution)/shard_map/ppermute | solution.py:439
  44.6 48.1 %collective-permute-start.12 = (bf16[768,768]{1,0:T(8,128)(2,1)}, bf16[768,768]{1,0:T(8,128)(2,1)}, u32[]{:S(2)}, u32[]{:S(2)}) collective-permute-start(bf16[768,768]{1,0:T(8,128)(2,1)} %bitcast.64), channel_id=1, source_target_pairs={{0,1},{1,0},{2,3},{3,2},{4,5},{5,4},{6,7},{7,6},{8,9},{9,8},{10,11... | collective-permute-start | bytes 3538952 | tf_op jit(solution)/shard_map/ppermute | solution.py:439
  90.5 31.2 %collective-permute-start.13 = (bf16[768,768]{1,0:T(8,128)(2,1)}, bf16[768,768]{1,0:T(8,128)(2,1)}, u32[]{:S(2)}, u32[]{:S(2)}) collective-permute-start(bf16[768,768]{1,0:T(8,128)(2,1)} %bitcast.65), channel_id=1, source_target_pairs={{0,2},{1,3},{2,0},{3,1},{4,6},{5,7},{6,4},{7,5},{8,10},{9,11},{10,... | collective-permute-start | bytes 3538952 | tf_op jit(solution)/shard_map/ppermute | solution.py:439
  103.4 39.8 %all-to-all-start = ((bf16[4,240,768]{2,1,0:T(8,128)(2,1)}), bf16[4,240,768]{2,1,0:T(8,128)(2,1)}, u32[]{:S(2)}, u32[]{:S(2)}) async-start(bf16[4,240,768]{2,1,0:T(8,128)(2,1)} %bitcast.57), calls=%async_computation | async-start | bytes 2949120 | tf_op jit(solution)/shard_map/all_to_all | solution.py:429
  107.8 119.9 %all-gather.7.cloned.1.call-start = ((), (), s32[]{:S(2)}) async-start(), calls=%async_computation.5 | async-start | bytes 4915200 | tf_op jit(solution)/shard_map/all_gather | solution.py:1116
  121.8 51.6 %collective-permute-start.15 = (bf16[240,768]{1,0:T(8,128)(2,1)}, bf16[240,768]{1,0:T(8,128)(2,1)S(1)}, u32[]{:S(2)}, u32[]{:S(2)}) collective-permute-start(bf16[240,768]{1,0:T(8,128)(2,1)} %get-tuple-element.238), channel_id=1, source_target_pairs={{0,8},{4,12},{8,0},{12,4},{16,24},{20,28},{24,16},{28,20},{1,9},{5... | collective-permute-start | bytes 1105928 | tf_op jit(solution)/shard_map/ppermute | solution.py:439
  121.9 51.9 %collective-permute-start.16 = (bf16[240,768]{1,0:T(8,128)(2,1)}, bf16[240,768]{1,0:T(8,128)(2,1)S(1)}, u32[]{:S(2)}, u32[]{:S(2)}) collective-permute-start(bf16[240,768]{1,0:T(8,128)(2,1)} %get-tuple-element.239), channel_id=1, source_target_pairs={{0,12},{4,8},{8,4},{12,0},{16,28},{20,24},{24,20},{28,16},{1,13},{... | collective-permute-start | bytes 1105928 | tf_op jit(solution)/shard_map/ppermute | solution.py:439
  125.2 48.5 %collective-permute-start.17 = (bf16[240,768]{1,0:T(8,128)(2,1)}, bf16[240,768]{1,0:T(8,128)(2,1)S(1)}, u32[]{:S(2)}, u32[]{:S(2)}) collective-permute-start(bf16[240,768]{1,0:T(8,128)(2,1)} %get-tuple-element.240), channel_id=1, source_target_pairs={{0,24},{4,28},{8,16},{12,20},{16,8},{20,12},{24,0},{28,4},{1,25},{... | collective-permute-start | bytes 1105928 | tf_op jit(solution)/shard_map/ppermute | solution.py:439
  127.2 46.6 %collective-permute-start.18 = (bf16[240,768]{1,0:T(8,128)(2,1)S(1)}, bf16[240,768]{1,0:T(8,128)(2,1)S(1)}, u32[]{:S(2)}, u32[]{:S(2)}) collective-permute-start(bf16[240,768]{1,0:T(8,128)(2,1)S(1)} %copy-done.26), channel_id=1, source_target_pairs={{0,28},{4,24},{8,20},{12,16},{16,12},{20,8},{24,4},{28,0},{1,29},{... | collective-permute-start | bytes 1105928 | tf_op jit(solution)/shard_map/ppermute | solution.py:439
  168.8 58.9 %all-to-all-start.2 = ((bf16[4,240,768]{2,1,0:T(8,128)(2,1)}), bf16[4,240,768]{2,1,0:T(8,128)(2,1)}, u32[]{:S(2)}, u32[]{:S(2)}) async-start(bf16[4,240,768]{2,1,0:T(8,128)(2,1)} %bitcast.71), calls=%async_computation.2 | async-start | bytes 2949120 | tf_op jit(solution)/shard_map/all_to_all | solution.py:429
  205.1 38.9 %collective-permute-start.19 = (bf16[240,768]{1,0:T(8,128)(2,1)}, bf16[240,768]{1,0:T(8,128)(2,1)S(1)}, u32[]{:S(2)}, u32[]{:S(2)}) collective-permute-start(bf16[240,768]{1,0:T(8,128)(2,1)} %get-tuple-element.243), channel_id=1, source_target_pairs={{0,8},{4,12},{8,0},{12,4},{16,24},{20,28},{24,16},{28,20},{1,9},{5... | collective-permute-start | bytes 1105928 | tf_op jit(solution)/shard_map/ppermute | solution.py:439
  206.3 37.7 %collective-permute-start.20 = (bf16[240,768]{1,0:T(8,128)(2,1)}, bf16[240,768]{1,0:T(8,128)(2,1)S(1)}, u32[]{:S(2)}, u32[]{:S(2)}) collective-permute-start(bf16[240,768]{1,0:T(8,128)(2,1)} %get-tuple-element.244), channel_id=1, source_target_pairs={{0,12},{4,8},{8,4},{12,0},{16,28},{20,24},{24,20},{28,16},{1,13},{... | collective-permute-start | bytes 1105928 | tf_op jit(solution)/shard_map/ppermute | solution.py:439
  208.3 35.7 %collective-permute-start.21 = (bf16[240,768]{1,0:T(8,128)(2,1)}, bf16[240,768]{1,0:T(8,128)(2,1)S(1)}, u32[]{:S(2)}, u32[]{:S(2)}) collective-permute-start(bf16[240,768]{1,0:T(8,128)(2,1)} %get-tuple-element.245), channel_id=1, source_target_pairs={{0,24},{4,28},{8,16},{12,20},{16,8},{20,12},{24,0},{28,4},{1,25},{... | collective-permute-start | bytes 1105928 | tf_op jit(solution)/shard_map/ppermute | solution.py:439
  210.2 33.9 %collective-permute-start.22 = (bf16[240,768]{1,0:T(8,128)(2,1)}, bf16[240,768]{1,0:T(8,128)(2,1)S(1)}, u32[]{:S(2)}, u32[]{:S(2)}) collective-permute-start(bf16[240,768]{1,0:T(8,128)(2,1)} %get-tuple-element.246), channel_id=1, source_target_pairs={{0,28},{4,24},{8,20},{12,16},{16,12},{20,8},{24,4},{28,0},{1,29},{... | collective-permute-start | bytes 1105928 | tf_op jit(solution)/shard_map/ppermute | solution.py:439
  245.1 71.0 %all-to-all-start.3 = ((bf16[8,240,768]{2,1,0:T(8,128)(2,1)}), bf16[8,240,768]{2,1,0:T(8,128)(2,1)S(1)}, u32[]{:S(2)}, u32[]{:S(2)}) async-start(bf16[8,240,768]{2,1,0:T(8,128)(2,1)} %bitcast.56), calls=%async_computation.3 | async-start | bytes 5898240 | tf_op jit(solution)/shard_map/all_to_all | solution.py:433
  275.6 30.5 %collective-permute-start.29 = (bf16[192,896]{1,0:T(8,128)(2,1)S(1)}, bf16[192,896]{1,0:T(8,128)(2,1)S(1)}, u32[]{:S(2)}, u32[]{:S(2)}) collective-permute-start(bf16[192,896]{1,0:T(8,128)(2,1)S(1)} %add_convert_fusion.3), channel_id=1, source_target_pairs={{0,2},{1,3},{2,0},{3,1},{4,6},{5,7},{6,4},{7,5},{8,10},{9,11},{10,... | collective-permute-start | bytes 1032200 | tf_op jit(solution)/shard_map/ppermute | solution.py:439
  276.3 39.8 %collective-permute-start.30 = (bf16[768,768]{1,0:T(8,128)(2,1)}, bf16[768,768]{1,0:T(8,128)(2,1)}, u32[]{:S(2)}, u32[]{:S(2)}) collective-permute-start(bf16[768,768]{1,0:T(8,128)(2,1)} %add_convert_fusion.1), channel_id=1, source_target_pairs={{0,2},{1,3},{2,0},{3,1},{4,6},{5,7},{6,4},{7,5},{8,10},{9,11},{10,... | collective-permute-start | bytes 3538952 | tf_op jit(solution)/shard_map/ppermute | solution.py:439
  318.8 29.3 %collective-permute-start.37 = (bf16[640,640]{1,0:T(8,128)(2,1)}, bf16[640,640]{1,0:T(8,128)(2,1)}, u32[]{:S(2)}, u32[]{:S(2)}) collective-permute-start(bf16[640,640]{1,0:T(8,128)(2,1)} %get-tuple-element.288.d2), channel_id=1, source_target_pairs={{0,2},{1,3},{2,0},{3,1},{4,6},{5,7},{6,4},{7,5},{8,10},{9,11},{10,... | collective-permute-start | bytes 2457608 | tf_op jit(solution)/shard_map/ppermute | solution.py:439
  319.5 30.6 %collective-permute-start.41 = (bf16[640,640]{1,0:T(8,128)(2,1)}, bf16[640,640]{1,0:T(8,128)(2,1)}, u32[]{:S(2)}, u32[]{:S(2)}) collective-permute-start(bf16[640,640]{1,0:T(8,128)(2,1)} %get-tuple-element.287.d1), channel_id=1, source_target_pairs={{0,1},{1,0},{2,3},{3,2},{4,5},{5,4},{6,7},{7,6},{8,9},{9,8},{10,11... | collective-permute-start | bytes 2457608 | tf_op jit(solution)/shard_map/ppermute | solution.py:439
  319.5 35.9 %collective-permute-start.42 = (bf16[640,640]{1,0:T(8,128)(2,1)}, bf16[640,640]{1,0:T(8,128)(2,1)}, u32[]{:S(2)}, u32[]{:S(2)}) collective-permute-start(bf16[640,640]{1,0:T(8,128)(2,1)} %get-tuple-element.289.d3), channel_id=1, source_target_pairs={{0,3},{1,2},{2,1},{3,0},{4,7},{5,6},{6,5},{7,4},{8,11},{9,10},{10,... | collective-permute-start | bytes 2457608 | tf_op jit(solution)/shard_map/ppermute | solution.py:439
  (65 other events, 624.6 us)
Sparse Core Ops, SparseCore 0:
  44.7 24.3 all-gather.4
  142.6 32.2 all-gather.6
